TPU v7x, 32 devices: a whole 2x2x4 slice. The times are simulated.
32 devices in a mesh: req: 16 (over z, y, x), col: 2 (over core).
Axes of the slice: x: 2, y: 2, z: 4, core: 2. Of those that a mesh axis runs over, the one named last changes fastest.
Arguments:
- tokens: bfloat16 [8192, 1024], P(('req', 'col')), may hold values from -6 to 6
- norm_gain_pair: float32 [2, 1024], replicated, may hold values from 0.5 to 1.5
- query_key_value_weight: bfloat16 [3, 1024, 1024], P(None, None, 'col'), may hold values from -1 to 1
- head_gate_weight: bfloat16 [2, 1024, 8], P(None, None, 'col'), may hold values from -0.1875 to 0.1875
- decay_logit_bias: float32 [8], P('col'), may hold values from -1 to 1024, as said below
- adapter_down_factor: bfloat16 [64, 1024, 16], P('col'), may hold values from -0.1875 to 0.1875
- adapter_up_factor: bfloat16 [64, 16, 1024], P(None, None, 'col'), may hold values from -1.5 to 1.5
- lengths: int32 [16, 2, 3], P('req'), may hold values from 1 to 128, 256 in all within a row
- request_adapter_index: int32 [16, 6], P('req'), may hold values from 0 to 63
- request_cache_index: int32 [16, 6], P('req'), may hold values from 0 to 127
- caches: bfloat16 [64, 8, 128, 128], P('req', 'col'), may hold values from -6 to 6
- head_output_weight: bfloat16 [1024, 1024], P('col'), may hold values from -0.1875 to 0.1875
- feedforward_weight: bfloat16 [3, 1024, 2816], P(None, None, 'col'), may hold values from -0.1875 to 0.1875
Outputs:
- layer_out: bfloat16 [8192, 1024], P(('req', 'col'))
Inputs may be any that keep to these rules, and one draw needn't show every extreme that they name: The 3 lengths of one device sum to 256, and the longest of them is exactly 128. `request_cache_index`: a value of 64 or more means that the request has no cached memory state. `decay_logit_bias`: at most the logarithm of 512.
All inputs are finite; a program needn't handle non-finite values.
Results may differ from a plain program's by a relative error of at most 0.015.
Values may be sent and summed in bfloat16 or wider, within the bound.
A program may use at most 192 MiB of HBM per device.

v0:
```python
import math

import jax
import jax.numpy as jnp
from jax import lax
from jax.sharding import PartitionSpec as P

epsilon = 1e-05


def rms_scale(values, gain):
    widened = values.astype(jnp.float32)
    factor = lax.rsqrt(jnp.mean(widened * widened, axis=-1, keepdims=True) + epsilon)
    return (widened * factor * gain).astype(jnp.bfloat16)


def on_device(
    tokens,
    norm_gain_pair,
    query_key_value_weight,
    head_gate_weight,
    decay_logit_bias,
    adapter_down_factor,
    adapter_up_factor,
    lengths,
    request_adapter_index,
    request_cache_index,
    caches,
    head_output_weight,
    feedforward_weight,
):
    tok_rows, width = tokens.shape
    col_count = lax.axis_size("col")
    group = tok_rows * col_count
    head_cols = query_key_value_weight.shape[2]
    local_heads = head_gate_weight.shape[2]
    head_size = head_cols // local_heads
    group_lengths = lengths[0].reshape(-1)
    scale = 1.0 / math.sqrt(head_size)
    normalized_rows = rms_scale(tokens, norm_gain_pair[0])
    gathered = lax.all_gather(normalized_rows, "col", axis=0, tiled=True)
    positions = jnp.arange(group, dtype=jnp.int32)
    ends = jnp.cumsum(group_lengths)
    starts = ends - group_lengths
    member = (
        (positions[:, None] >= starts[None, :]) & (positions[:, None] < ends[None, :])
    ).astype(jnp.float32)
    segment = jnp.sum((positions[:, None] >= ends[None, :]).astype(jnp.int32), axis=1)
    projected = jnp.einsum(
        "td,kdc->ktc", gathered, query_key_value_weight, preferred_element_type=jnp.float32
    )
    token_segment = lax.all_gather(adapter_down_factor, "col", axis=0, tiled=True)
    numbers = jnp.arange(token_segment.shape[0], dtype=jnp.int32)
    select = (request_adapter_index[0][:, None] == numbers[None, :]).astype(jnp.bfloat16)
    chosen = jnp.einsum(
        "sa,adr->sdr", select, token_segment, preferred_element_type=jnp.float32
    ).astype(jnp.bfloat16)
    per_request = jnp.einsum("td,sdr->tsr", gathered, chosen, preferred_element_type=jnp.float32)
    low_rank_delta = jnp.sum(member[:, :, None] * per_request, axis=1)
    low_rank_delta = low_rank_delta.astype(jnp.bfloat16)
    adapter_onehot = (
        request_adapter_index[0][:, None]
        == jnp.arange(adapter_up_factor.shape[0], dtype=jnp.int32)[None, :]
    ).astype(jnp.bfloat16)
    up_chosen = jnp.einsum(
        "gq,qjl->gjl", adapter_onehot, adapter_up_factor, preferred_element_type=jnp.float32
    ).astype(jnp.bfloat16)
    delta_all = jnp.einsum(
        "tr,src->tsc", low_rank_delta, up_chosen, preferred_element_type=jnp.float32
    )
    delta = jnp.sum(member[:, :, None] * delta_all, axis=1)
    queries = (projected[0] + delta).astype(jnp.bfloat16).reshape(group, local_heads, head_size)
    keys = projected[1].astype(jnp.bfloat16).reshape(group, local_heads, head_size)
    values = projected[2].astype(jnp.bfloat16).reshape(group, local_heads, head_size)
    gate_terms = jnp.einsum(
        "td,kdh->kth", gathered, head_gate_weight, preferred_element_type=jnp.float32
    )
    log_keep = jax.nn.log_sigmoid(gate_terms[0] + decay_logit_bias[None, :])
    mix_gate = jax.nn.sigmoid(gate_terms[1])
    running = jnp.cumsum(log_keep, axis=0)
    before = running - log_keep
    start_hot = (positions[None, :] == starts[:, None]).astype(jnp.float32)
    start_level = jnp.sum(start_hot[:, :, None] * before[None, :, :], axis=1)
    level = running - jnp.sum(member[:, :, None] * start_level[None, :, :], axis=1)
    token_segment = lax.all_gather(caches, "req", axis=0, tiled=True)
    numbers = jnp.arange(token_segment.shape[0], dtype=jnp.int32)
    select = (request_cache_index[0][:, None] == numbers[None, :]).astype(jnp.bfloat16)
    states = jnp.einsum(
        "sn,nhij->shij", select, token_segment, preferred_element_type=jnp.float32
    ).astype(jnp.bfloat16)
    from_state = jnp.einsum("thi,shij->tshj", queries, states, preferred_element_type=jnp.float32)
    carried = jnp.sum(member[:, :, None, None] * from_state, axis=1) * jnp.exp(level)[:, :, None]
    block = min(512, group)

    def one_block(index):
        begin = index * block
        scores = (
            jnp.einsum("qhd,khd->hqk", queries, keys, preferred_element_type=jnp.float32) * scale
        )
        q_pos = begin + jnp.arange(block, dtype=jnp.int32)
        allowed = (segment[:, None] == segment[None, :]) & (positions[None, :] <= q_pos[:, None])
        masked = jnp.where(allowed[None], scores, -jnp.inf)
        peak = jnp.max(masked, axis=2, keepdims=True)
        weights = jnp.exp(masked - peak)
        probs = (weights / jnp.sum(weights, axis=2, keepdims=True)).astype(jnp.bfloat16)
        attended = jnp.einsum("hqk,khd->qhd", probs, values, preferred_element_type=jnp.float32)
        gap = jnp.where(allowed[None], running.T[:, :, None] - running.T[:, None, :], -jnp.inf)
        memory_w = (scores * jnp.exp(gap)).astype(jnp.bfloat16)
        recalled = jnp.einsum("hqk,khd->qhd", memory_w, values, preferred_element_type=jnp.float32)
        recalled = recalled + carried
        factor = lax.rsqrt(jnp.mean(recalled * recalled, axis=2, keepdims=True) + epsilon)
        combined = attended + mix_gate[:, :, None] * recalled * factor
        return combined.astype(jnp.bfloat16).reshape(block, head_cols)

    blocks = lax.map(one_block, jnp.arange(group // block, dtype=jnp.int32))
    head_out = blocks.reshape(group, head_cols)
    attn_proj = lax.psum_scatter(
        jnp.dot(head_out, head_output_weight, preferred_element_type=jnp.float32),
        "col",
        scatter_dimension=0,
        tiled=True,
    )
    mixed = (tokens.astype(jnp.float32) + attn_proj).astype(jnp.bfloat16)
    normed_two = rms_scale(mixed, norm_gain_pair[1])
    token_segment = lax.all_gather(feedforward_weight, "col", axis=2, tiled=True)
    gate_up = jnp.einsum(
        "td,kdf->ktf", normed_two, token_segment[:2], preferred_element_type=jnp.float32
    )
    hidden = (jax.nn.silu(gate_up[0]) * gate_up[1]).astype(jnp.bfloat16)
    feed = jnp.einsum("tf,df->td", hidden, token_segment[2], preferred_element_type=jnp.float32)
    return (mixed.astype(jnp.float32) + feed).astype(jnp.bfloat16)


def solution(mesh):
    placed = (
        P(("req", "col"), None),
        P(),
        P(None, None, "col"),
        P(None, None, "col"),
        P("col"),
        P("col", None, None),
        P(None, None, "col"),
        P("req", None, None),
        P("req", None),
        P("req", None),
        P("req", "col", None, None),
        P("col", None),
        P(None, None, "col"),
    )
    return jax.shard_map(
        on_device, mesh=mesh, in_specs=placed, out_specs=P(("req", "col"), None), check_vma=False
    )
```

profile of v0, /device:TPU:0, one launch (start us, length us, event | category | flops | bytes accessed | tf_op | source)
XLA Modules:
  0.0 233.7 jit_solution(18112921878536416983)
XLA Ops:
  6.5 1.5 fusion.87
  8.0 1.2 fusion.38
  9.2 2.0 fusion.40
  11.3 0.7 all-gather.7.cloned.1.call-update
  12.1 0.7 all-gather.9.cloned.1.call-update
  12.8 0.8 reshape.275
  13.6 0.8 reshape_squeeze.3
  14.6 0.7 fusion.62
  15.6 2.4 %convolution_convert_fusion = bf16[6,16,512]{2,0,1:T(8,128)(2,1)S(1)} fusion(bf16[64,16,512]{2,1,0:T(8,128)(2,1)} %param.19, s32[6]{0:T(128)} %bitcast.134), kind=kOutput, calls=%fused_computation.42 | convolution fusion | flops 6340992 | bytes 1146904 | tf_op jit(solution)/shard_map/gq,qjl->gjl/dot_general | solution.py:65
  18.0 5.2 %all-gather.5.cloned.1.call-done = bf16[512,1024]{1,0:T(8,128)(2,1)} async-done(((bf16[256,1024]{1,0:T(8,128)(2,1)}), bf16[512,1024]{1,0:T(8,128)(2,1)}) %all-gather.5.cloned.1.call-update) | async-done | bytes 1048592 | tf_op jit(solution)/shard_map/all_gather | solution.py:41
  23.2 1.6 convolution_bitcast_fusion.1
  25.4 1.3 fusion.84
  26.7 1.3 reshape.277
  28.0 3.1 %reduce-window.18 = f32[4,4,128]{2,1,0:T(4,128)} reduce-window(f32[4,4,128]{2,1,0:T(4,128)} %reshape.277, f32[]{:T(128)} %constant.42.clone.1), window={size=1x1x128 pad=0_0x0_0x127_0}, to_apply=%region_7.8 | reduce-window | flops 260096 | bytes 16388 | tf_op jit(solution)/shard_map/reduce-window.1
  31.1 1.4 slice_reduce_fusion
  32.5 1.4 reduce-window.19
  34.0 3.4 %fusion.88 = (bf16[3,512,512]{1,2,0:T(8,128)(2,1)S(1)}, f32[3,512,512]{1,2,0:T(8,128)S(1)}) fusion(bf16[3,1024,512]{2,1,0:T(8,128)(2,1)S(1)} %copy-done, bf16[512,1024]{1,0:T(8,128)(2,1)} %all-gather.5.cloned.1.call-done), kind=kOutput, calls=%fused_computation.113 | convolution fusion | flops 1611399168 | bytes 8912896 | tf_op jit(solution)/shard_map/td,kdc->ktc/dot_general | solution.py:49
  39.7 1.1 fusion.86
  40.8 3.9 %fusion.35 = bf16[6,1024,16]{1,0,2:T(8,128)(2,1)S(1)} fusion(bf16[64,1024,16]{1,2,0:T(8,128)(2,1)} %all-gather.7.cloned.1.call-done, s32[6]{0:T(128)S(1)} %bitcast.135), kind=kOutput, calls=%fused_computation.41 | convolution fusion | flops 12681600 | bytes 2293784 | tf_op jit(solution)/shard_map/sa,adr->sdr/dot_general | solution.py:55
  45.3 1.0 multiply_reduce_fusion
  46.9 4.7 %fusion.89 = (f32[4,512]{1,0:T(4,128)S(1)}, f32[4,512,512]{1,2,0:T(8,128)}) fusion(pred[512,512]{0,1:T(8,128)(4,1)S(1)} %fusion.48, bf16[512,4,128]{0,2,1:T(8,128)(2,1)S(1)} %add_convert_fusion, bf16[512,4,128]{0,2,1:T(8,128)(2,1)} %bitcast.128), kind=kOutput, calls=%fused_computation.114 | convolution fusion | flops 272630272 | bytes 5513216 | tf_op jit(solution)/shard_map/while/body/eval_jaxpr/sub | solution.py:104
  51.6 101.7 %all-gather.9.cloned.1.call-done = bf16[64,4,128,128]{3,2,1,0:T(8,128)(2,1)} async-done(((bf16[4,4,128,128]{3,2,1,0:T(8,128)(2,1)}), bf16[64,4,128,128]{3,2,1,0:T(8,128)(2,1)}) %all-gather.9.cloned.1.call-update) | async-done | bytes 8388624 | tf_op jit(solution)/shard_map/all_gather | solution.py:85
  153.3 8.1 %fusion.20 = bf16[6,4,128,128]{3,0,2,1:T(8,128)(2,1)S(1)} fusion(bf16[64,4,128,128]{3,2,1,0:T(8,128)(2,1)} %all-gather.9.cloned.1.call-done, s32[6]{0:T(128)S(1)} %bitcast.138), kind=kOutput, calls=%fused_computation.33 | convolution fusion | flops 50725248 | bytes 9175064 | tf_op jit(solution)/shard_map/sn,nhij->shij/dot_general | solution.py:88
  161.5 2.0 fusion.5
  163.5 4.1 %multiply_reduce_fusion.1 = (f32[512,4]{0,1:T(4,128)S(1)}, f32[512,4,128]{0,2,1:T(8,128)}) fusion(f32[512,4,128]{0,2,1:T(8,128)} %fusion.5, f32[512,4]{0,1:T(4,128)S(1)} %copy-done.12, bf16[512,4,128]{0,2,1:T(8,128)(2,1)S(1)} %bitcast.126, f32[4,512]{1,0:T(4,128)S(1)} %bitcast.132, pred[512,512]{0,1:T(8,128)(4,1)S(1)} %fusion.48, ...), kind=kOutput, calls=%fused_computation.54 | convolution fusion | flops 543160320 | bytes 3956736 | tf_op jit(solution)/shard_map/while/body/eval_jaxpr/hqk,khd->qhd/dot_general | solution.py:109
  167.6 3.1 %fusion.31 = bf16[512,4,128]{0,2,1:T(8,128)(2,1)S(1)} fusion(bf16[512,4,128]{0,2,1:T(8,128)(2,1)S(1)} %bitcast.127, f32[4,512,512]{1,2,0:T(8,128)} %get-tuple-element.44, f32[4,512]{1,0:T(4,128)S(1)} %get-tuple-element.42, f32[512,4,128]{0,2,1:T(8,128)} %get-tuple-element.46, f32[512,4]{0,1:T(4,128)S(1)} %add_rsqrt_fusion, f32[512,4]{0,1:T(4,128)S(1)} %copy-done.14), kind=kOutput, calls=%fused_computation.39 | convolution fusion | flops 271581184 | bytes 6316032 | tf_op jit(solution)/shard_map/while/body/eval_jaxpr/hqk,khd->qhd/dot_general | solution.py:106
  170.7 2.1 fusion.93
  173.4 7.3 %reduce-scatter.2.cloned.1.call-done = f32[256,1024]{1,0:T(8,128)} async-done(((f32[512,1024]{1,0:T(8,128)}), f32[256,1024]{1,0:T(8,128)}) %reduce-scatter.2.cloned.1.call-update) | async-done | bytes 1048592 | tf_op jit(solution)/shard_map/reduce_scatter | solution.py:117
  180.8 1.5 fusion.42
  182.2 33.4 %all-gather.11.cloned.1.call-done = bf16[3,1024,2816]{2,1,0:T(8,128)(2,1)} async-done(((bf16[3,1024,1408]{2,1,0:T(8,128)(2,1)}), bf16[3,1024,2816]{2,1,0:T(8,128)(2,1)}) %all-gather.11.cloned.1.call-update) | async-done | bytes 17301520 | tf_op jit(solution)/shard_map/all_gather | solution.py:125
  215.7 6.1 %fusion.7 = f32[2,256,2816]{2,1,0:T(8,128)S(1)} fusion(bf16[3,1024,2816]{2,1,0:T(8,128)(2,1)} %all-gather.11.cloned.1.call-done, bf16[256,1024]{1,0:T(8,128)(2,1)S(1)} %get-tuple-element.24, f32[1024]{0:T(1024)S(1)} %bitcast.133, f32[256]{0:T(256)S(1)} %add_rsqrt_fusion.1), kind=kOutput, calls=%fused_computation.10 | convolution fusion | flops 2953838592 | bytes 17830912 | tf_op jit(solution)/shard_map/td,kdf->ktf/dot_general | solution.py:126
  221.8 5.4 %fusion.32 = bf16[256,1024]{1,0:T(8,128)(2,1)} fusion(bf16[3,1024,2816]{2,1,0:T(8,128)(2,1)} %all-gather.11.cloned.1.call-done, f32[2,256,2816]{2,1,0:T(8,128)S(1)} %fusion.7, bf16[256,1024]{1,0:T(8,128)(2,1)} %copy-done.7), kind=kOutput, calls=%fused_computation.40 | convolution fusion | flops 1481506816 | bytes 12582912 | tf_op jit(solution)/shard_map/tf,df->td/dot_general | solution.py:130
  (70 shorter events, 5.4 us)
Async XLA Ops:
  6.5 27.4 %copy-start = (bf16[3,1024,512]{2,1,0:T(8,128)(2,1)S(1)}, bf16[3,1024,512]{2,1,0:T(8,128)(2,1)}, u32[]{:S(2)}) copy-start(bf16[3,1024,512]{2,1,0:T(8,128)(2,1)} %param.15) | copy-start | bytes 9437188
  6.5 16.6 %all-gather.5.cloned.1.call-start = ((), (), s32[]{:S(2)}) async-start(), calls=%async_computation.1 | async-start | bytes 1572864 | tf_op jit(solution)/shard_map/all_gather | solution.py:41
  11.3 29.5 %all-gather.7.cloned.1.call-start = ((), (), s32[]{:S(2)}) async-start(), calls=%async_computation.2 | async-start | bytes 3145728 | tf_op jit(solution)/shard_map/all_gather | solution.py:52
  12.0 141.3 %all-gather.9.cloned.1.call-start = ((), (), s32[]{:S(2)}) async-start(), calls=%async_computation.3 | async-start | bytes 8912896 | tf_op jit(solution)/shard_map/all_gather | solution.py:85
  12.8 168.0 %reduce-scatter.2.cloned.1.call-start = ((), (), s32[]{:S(2)}) async-start(), calls=%async_computation.4 | async-start | bytes 3145728 | tf_op jit(solution)/shard_map/reduce_scatter | solution.py:117
  24.8 0.6 copy-start.8
  34.0 3.5 %copy-start.10 = (f32[4,4,128]{2,1,0:T(4,128)S(1)}, f32[4,4,128]{2,1,0:T(4,128)}, u32[]{:S(2)}) copy-start(f32[4,4,128]{2,1,0:T(4,128)} %reduce-window.18) | copy-start | bytes 24580
  34.0 3.5 %copy-start.13 = (f32[4,5]{1,0:T(4,128)S(1)}, f32[4,5]{1,0:T(4,128)}, u32[]{:S(2)}) copy-start(f32[4,5]{1,0:T(4,128)} %reduce-window.19) | copy-start | bytes 244
  34.0 4.2 %copy-start.9 = (f32[2,512,4]{1,2,0:T(4,128)S(1)}, f32[2,512,4]{1,2,0:T(4,128)}, u32[]{:S(2)}) copy-start(f32[2,512,4]{1,2,0:T(4,128)} %copy-done.8) | copy-start | bytes 49156
  34.0 4.2 %copy-start.18 = (f32[4]{0:T(128)S(1)}, f32[4]{0:T(128)}, u32[]{:S(2)}) copy-start(f32[4]{0:T(128)} %param.17) | copy-start | bytes 52
  34.0 4.3 %copy-start.11 = (f32[6,512]{1,0:T(8,128)S(1)}, f32[6,512]{1,0:T(8,128)}, u32[]{:S(2)}) copy-start(f32[6,512]{1,0:T(8,128)} %fusion.62) | copy-start | bytes 36868
  37.4 3.4 %copy-start.17 = (s32[1,6]{1,0:T(1,128)S(1)}, s32[1,6]{1,0:T(1,128)}, u32[]{:S(2)}) copy-start(s32[1,6]{1,0:T(1,128)} %param.21) | copy-start | bytes 76
  37.4 7.4 %copy-start.3 = (bf16[512,1024]{1,0:T(8,128)(2,1)S(1)}, bf16[512,1024]{1,0:T(8,128)(2,1)}, u32[]{:S(2)}) copy-start(bf16[512,1024]{1,0:T(8,128)(2,1)} %all-gather.5.cloned.1.call-done) | copy-start | bytes 3145732
  46.9 106.4 %copy-start.19 = (s32[1,6]{1,0:T(1,128)S(1)}, s32[1,6]{1,0:T(1,128)}, u32[]{:S(2)}) copy-start(s32[1,6]{1,0:T(1,128)} %param.22) | copy-start | bytes 76
  161.4 2.0 copy-start.5
  161.4 2.0 copy-start.6
  161.4 2.0 copy-start.12
  161.4 2.0 copy-start.15
  163.5 4.1 %copy-start.14 = (f32[512,4]{0,1:T(4,128)S(1)}, f32[512,4]{0,1:T(4,128)}, u32[]{:S(2)}) copy-start(f32[512,4]{0,1:T(4,128)} %fusion.69) | copy-start | bytes 24580
  167.6 3.1 %copy-start.4 = (bf16[512,1024]{1,0:T(8,128)(2,1)S(1)}, bf16[512,1024]{1,0:T(8,128)(2,1)}, u32[]{:S(2)}) copy-start(bf16[512,1024]{1,0:T(8,128)(2,1)} %param.24) | copy-start | bytes 3145732
  172.8 8.0 %copy-start.2 = (bf16[256,1024]{1,0:T(8,128)(2,1)S(1)}, bf16[256,1024]{1,0:T(8,128)(2,1)}, u32[]{:S(2)}) copy-start(bf16[256,1024]{1,0:T(8,128)(2,1)} %param.13) | copy-start | bytes 1572868
  172.8 42.8 %copy-start.16 = (f32[1,1024]{1,0:T(1,128)S(1)}, f32[1,1024]{1,0:T(1,128)}, u32[]{:S(2)}) copy-start(f32[1,1024]{1,0:T(1,128)} %get-tuple-element.27) | copy-start | bytes 12292
  172.8 42.8 %all-gather.11.cloned.1.call-start = ((), (), s32[]{:S(2)}) async-start(), calls=%async_computation.5 | async-start | bytes 25952256 | tf_op jit(solution)/shard_map/all_gather | solution.py:125
  182.2 33.4 %copy-start.7 = (bf16[256,1024]{1,0:T(8,128)(2,1)}, bf16[256,1024]{1,0:T(8,128)(2,1)S(1)}, u32[]{:S(2)}) copy-start(bf16[256,1024]{1,0:T(8,128)(2,1)S(1)} %get-tuple-element.24) | copy-start | bytes 1572868
  221.8 5.4 %copy-start.1 = (bf16[3,1024,512]{2,1,0:T(8,128)(2,1)S(1)}, bf16[3,1024,512]{2,1,0:T(8,128)(2,1)}, u32[]{:S(2)}) copy-start(bf16[3,1024,512]{2,1,0:T(8,128)(2,1)} %param.15) | copy-start | bytes 9437188
Sparse Core Ops, SparseCore 0:
  11.4 11.7 all-gather.4
  24.7 11.7 all-gather.6
  39.3 113.9 all-gather.8
  172.9 7.7 reduce-scatter.1
  182.2 33.3 all-gather.10
where the time goes:
time: 234 us
  waiting for transfers between devices  150 us (64%)
  matrix products  48.3 us (21%)
  other arithmetic  13.6 us (6%)
  between operations  13.4 us (6%)
  local copies, waits for them, and re-layouts  8.62 us (4%)
    all_gather x1, waiting for transfers between devices, on_device(): token_segment = lax.all_gather(caches, 'req', axis=0, tiled=True)  102 us
    all_gather x1, waiting for transfers between devices, on_device(): lax.all_gather(feedforward_weight, 'col', axis=2, tiled=True)  33.4 us
    dot_general x1, matrix products, on_device(): jnp.einsum('sn,nhij->shij', select, token_segment, preferred_element_type...  8.12 us
    reduce_scatter x1, waiting for transfers between devices, on_device(): lax.psum_scatter(jnp.dot(head_out, head_output_weight, preferred_element_...  7.34 us
    dot_general x1, matrix products, on_device(): jnp.einsum('td,kdf->ktf', normed_two, token_segment[:2], preferred_elemen...  6.11 us
    another operation x4, other arithmetic  6 us
    dot_general x1, matrix products, on_device(): jnp.einsum('tf,df->td', hidden, token_segment[2], preferred_element_type=...  5.37 us
    all_gather x1, waiting for transfers between devices, on_device(): gathered = lax.all_gather(normalized_rows, 'col', axis=0, tiled=True)  5.16 us
  transfers between devices with their start and end apart: 5, of which 4 were waited for; matrix products, arithmetic and copies ran while one was open for 15% of the time, Pallas kernels for 0%

commit v1 on v0

v1 whole, which is shorter than its diff:
```python
import functools
import math

import jax
import jax.numpy as jnp
from jax import lax
from jax.experimental import pallas as pl
from jax.experimental.pallas import tpu as pltpu
from jax.sharding import PartitionSpec as P

epsilon = 1e-05
MESH = pl.DeviceIdType.MESH


def rms_scale(values, gain):
    widened = values.astype(jnp.float32)
    factor = lax.rsqrt(jnp.mean(widened * widened, axis=-1, keepdims=True) + epsilon)
    return (widened * factor * gain).astype(jnp.bfloat16)


def mix_kernel(
    n, seqs, rank, heads, dh,
    lens_ref, idx_ref, tok_ref, gain_ref, aux_ref, up_ref, bias_ref, qkv_ref, cache_ref, wo_ref, ff_ref,
    out_ref, wo_other, ff_other,
    wq, auxr, upr, biasr, r1, idxb, idxs, stage, r2, q_s, k_s, v_s, att_s, intra_s,
    s1, t1, si, ti, s2, t2, sp, tp, lsem,
):
    g = lax.axis_index("req")
    c = lax.axis_index("col")
    other = 1 - c
    me = g * 2 + c
    total = n * 2
    own = cache_ref.shape[0]
    rows = tok_ref.shape[0]
    half = heads // 2
    f32, bf16 = jnp.float32, jnp.bfloat16

    barrier = pltpu.get_barrier_semaphore()

    def greet(k, carry):
        d = lax.rem(me + k, total)
        pl.semaphore_signal(barrier, inc=1, device_id=(d // 2, lax.rem(d, 2)), device_id_type=MESH)
        return carry

    local_w = pltpu.make_async_copy(qkv_ref, wq.at[c], lsem.at[0])
    local_w.start()
    local_c = pltpu.make_async_copy(cache_ref.at[:, g], r1.at[pl.ds(own * g, own)], lsem.at[1])
    local_c.start()
    local_i = pltpu.make_async_copy(idx_ref, idxb.at[g], lsem.at[2])
    local_i.start()

    lax.fori_loop(1, total, greet, 0)
    pl.semaphore_wait(barrier, total - 1)

    def cache_copy(p, slot, sem):
        return pltpu.make_async_remote_copy(
            src_ref=cache_ref.at[:, p], dst_ref=r1.at[pl.ds(own * slot, own)],
            send_sem=s1.at[p], recv_sem=t1.at[sem], device_id=(p, c), device_id_type=MESH)

    def index_copy(p, slot):
        return pltpu.make_async_remote_copy(
            src_ref=idx_ref, dst_ref=idxb.at[slot],
            send_sem=si.at[p], recv_sem=ti.at[slot], device_id=(p, c), device_id_type=MESH)

    def first(k, carry):
        p = lax.rem(g + k, n)
        index_copy(p, g).start()
        cache_copy(p, g, g).start()
        return carry

    lax.fori_loop(1, n, first, 0)

    def pair(src, dst, i):
        return pltpu.make_async_remote_copy(
            src_ref=src, dst_ref=dst, send_sem=sp.at[i], recv_sem=tp.at[i],
            device_id=(g, other), device_id_type=MESH)

    pairs = [
        pair(aux_ref.at[other], auxr, 0),
        pair(bias_ref, biasr, 1),
        pair(up_ref.at[other], upr.at[c], 2),
        pair(qkv_ref, wq.at[c], 3),
        pair(wo_ref, wo_other, 4),
        pair(ff_ref, ff_other, 5),
    ]
    for one in pairs:
        one.start()
    upr[c] = up_ref[c]

    x = tok_ref[...].astype(f32)
    factor = lax.rsqrt(jnp.mean(x * x, axis=-1, keepdims=True) + epsilon)
    normed = (x * factor * gain_ref[0:1, :]).astype(bf16)

    first_end = lens_ref[c * seqs]
    ends = [first_end]
    for j in range(1, seqs - 1):
        ends.append(ends[-1] + lens_ref[c * seqs + j])

    def segment_of(shape, axis):
        pos = lax.broadcasted_iota(jnp.int32, shape, axis)
        seg = jnp.zeros(shape, jnp.int32)
        for e in ends:
            seg = seg + (pos >= e).astype(jnp.int32)
        return pos, seg

    q_pos, q_seg = segment_of((rows, rows), 0)
    k_pos, k_seg = segment_of((rows, rows), 1)
    allowed = (q_seg == k_seg) & (k_pos <= q_pos)
    _, seg_wide = segment_of((rows, 128), 0)

    pairs[0].wait_recv()
    pairs[1].wait_recv()
    aux = aux_ref[c] + auxr[...]
    bias = bias_ref[0:1, :] + biasr[0:1, :]
    terms = jnp.dot(normed, aux, preferred_element_type=f32)
    lane = lax.broadcasted_iota(jnp.int32, (rows, 128), 1)
    mine = lane // rank == seg_wide
    low = jnp.where(mine, terms, 0.0).astype(bf16)
    shifted = terms + bias
    log_keep = jnp.minimum(shifted, 0.0) - jnp.log1p(jnp.exp(-jnp.abs(shifted)))
    mix_gate = 1.0 / (1.0 + jnp.exp(-terms))
    ones = allowed.astype(f32).astype(bf16)
    part = log_keep.astype(bf16)
    level = jnp.dot(ones, part, preferred_element_type=f32)
    rest = log_keep - part.astype(f32)
    part = rest.astype(bf16)
    level = level + jnp.dot(ones, part, preferred_element_type=f32)
    part = (rest - part.astype(f32)).astype(bf16)
    level = level + jnp.dot(ones, part, preferred_element_type=f32)
    level_t = jnp.transpose(level)
    base = seqs * rank

    pairs[2].wait_recv()
    pairs[3].wait_recv()
    local_w.wait()
    width = half * dh
    for b in range(2):
        cols = pl.ds(b * width, width)
        q = jnp.dot(normed, wq[b, 0], preferred_element_type=f32)
        q_s[:, cols] = (q + jnp.dot(low, upr[b], preferred_element_type=f32)).astype(bf16)
        k_s[:, cols] = jnp.dot(normed, wq[b, 1], preferred_element_type=f32).astype(bf16)
        v_s[:, cols] = jnp.dot(normed, wq[b, 2], preferred_element_type=f32).astype(bf16)

    local_c.wait()
    local_i.wait()

    def first_wait(k, carry):
        p = lax.rem(g + k, n)
        index_copy(p, p).wait_recv()
        cache_copy(p, p, p).wait_recv()
        return carry

    lax.fori_loop(1, n, first_wait, 0)
    to_smem = pltpu.make_async_copy(idxb, idxs, lsem.at[3])
    to_smem.start()
    to_smem.wait()

    def pick(p):
        for b in range(2):
            for j in range(seqs):
                i = idxs[p, 0, b * seqs + j]
                piece = r1[jnp.minimum(i, own * n - 1)]
                stage[p, b, j] = jnp.where(i < own * n, piece, jnp.zeros_like(piece))

    def second_copy(d, slot_c, slot_g):
        return pltpu.make_async_remote_copy(
            src_ref=stage.at[d // 2, lax.rem(d, 2)], dst_ref=r2.at[slot_c, slot_g],
            send_sem=s2.at[d], recv_sem=t2.at[slot_c * n + slot_g],
            device_id=(d // 2, lax.rem(d, 2)), device_id_type=MESH)

    def second(k, carry):
        p = lax.rem(g + k, n)
        pick(p)
        second_copy(p * 2, c, g).start()
        second_copy(p * 2 + 1, c, g).start()
        return carry

    lax.fori_loop(1, n, second, 0)
    pick(g)
    second_copy(g * 2 + other, c, g).start()
    keep = pltpu.make_async_copy(stage.at[g, c], r2.at[c, g], lsem.at[4])
    keep.start()

    scale = 1.0 / math.sqrt(dh)
    for h in range(heads):
        cols = pl.ds(h * dh, dh)
        scores = lax.dot_general(
            q_s[:, cols], k_s[:, cols], (((1,), (1,)), ((), ())), preferred_element_type=f32) * scale
        masked = jnp.where(allowed, scores, -jnp.inf)
        peak = jnp.max(masked, axis=1, keepdims=True)
        weights = jnp.exp(masked - peak)
        probs = (weights / jnp.sum(weights, axis=1, keepdims=True)).astype(bf16)
        att_s[:, cols] = jnp.dot(probs, v_s[:, cols], preferred_element_type=f32)
        gap = jnp.where(allowed, level[:, base + h:base + h + 1] - level_t[base + h:base + h + 1, :], -jnp.inf)
        memory_w = (scores * jnp.exp(gap)).astype(bf16)
        intra_s[:, cols] = jnp.dot(memory_w, v_s[:, cols], preferred_element_type=f32)

    keep.wait()

    def second_wait(k, carry):
        d = lax.rem(me + k, total)
        second_copy(d, lax.rem(d, 2), d // 2).wait_recv()
        return carry

    lax.fori_loop(1, total, second_wait, 0)

    per_head = n // half
    for h in range(heads):
        cols = pl.ds(h * dh, dh)
        q = q_s[:, cols]
        carried = jnp.zeros((rows, dh), f32)
        for j in range(seqs):
            state = r2[h // half, (h % half) * per_head:(h % half + 1) * per_head, j]
            state = state.astype(f32).reshape(dh, dh).astype(bf16)
            carried = jnp.where(seg_wide == j, jnp.dot(q, state, preferred_element_type=f32), carried)
        recalled = carried * jnp.exp(level[:, base + h:base + h + 1]) + intra_s[:, cols]
        factor = lax.rsqrt(jnp.mean(recalled * recalled, axis=1, keepdims=True) + epsilon)
        gate = mix_gate[:, base + heads + h:base + heads + h + 1]
        out_ref[:, cols] = (att_s[:, cols] + gate * recalled * factor).astype(bf16)

    def drain_first(k, carry):
        p = lax.rem(g + k, n)
        index_copy(p, g).wait_send()
        cache_copy(p, g, g).wait_send()
        return carry

    lax.fori_loop(1, n, drain_first, 0)

    def drain_second(k, carry):
        second_copy(lax.rem(me + k, total), c, g).wait_send()
        return carry

    lax.fori_loop(1, total, drain_second, 0)
    for one in pairs:
        one.wait_send()
    pairs[4].wait_recv()
    pairs[5].wait_recv()


def on_device(
    tokens, norm_gain_pair, query_key_value_weight, head_gate_weight, decay_logit_bias,
    adapter_down_factor, adapter_up_factor, lengths, request_adapter_index, request_cache_index,
    caches, head_output_weight, feedforward_weight,
):
    n = lax.axis_size("req")
    c = lax.axis_index("col")
    rows, width = tokens.shape
    seqs = lengths.shape[2]
    adapters, _, rank = adapter_down_factor.shape
    local_heads = head_gate_weight.shape[2]
    heads = 2 * local_heads
    head_cols = query_key_value_weight.shape[2]
    dh = head_cols // local_heads
    own = caches.shape[0]
    piece = local_heads * dh // n
    bf16 = jnp.bfloat16

    which = request_adapter_index[0]
    local = which - c * adapters
    held = (local >= 0) & (local < adapters)
    picked = [
        jnp.where(held[s], lax.dynamic_index_in_dim(
            adapter_down_factor, jnp.clip(local[s], 0, adapters - 1), 0, keepdims=False), 0).astype(bf16)
        for s in range(2 * seqs)
    ]
    used = seqs * rank
    gates = jnp.zeros((2, width, 2, local_heads), bf16)
    gates = jnp.where(jnp.arange(2)[None, None, :, None] == c, head_gate_weight[:, :, None, :], gates)
    gates = gates.reshape(2, width, heads)
    filler = jnp.zeros((width, 128 - used - 2 * heads), bf16)
    aux = jnp.stack([
        jnp.concatenate(picked[b * seqs:(b + 1) * seqs] + [gates[0], gates[1], filler], axis=1) for b in range(2)])
    up = [lax.dynamic_index_in_dim(adapter_up_factor, which[s], 0, keepdims=False) for s in range(2 * seqs)]
    blank = jnp.zeros((128 - used, head_cols), bf16)
    up = jnp.stack([jnp.concatenate(up[b * seqs:(b + 1) * seqs] + [blank], axis=0) for b in range(2)])
    bias = jnp.where(jnp.arange(2)[:, None] == c, decay_logit_bias[None, :], 0.0).reshape(heads)
    bias = jnp.broadcast_to(jnp.pad(bias, (used, 128 - used - heads))[None], (8, 128))
    index = jnp.broadcast_to(jnp.pad(request_cache_index[0], (0, 128 - 2 * seqs))[None], (8, 128))

    vmem = pl.BlockSpec(memory_space=pltpu.VMEM)
    smem = pl.BlockSpec(memory_space=pltpu.SMEM)
    hbm = pl.BlockSpec(memory_space=pl.ANY)
    dma = pltpu.SemaphoreType.DMA
    head_out, wo_other, ff_other = pl.pallas_call(
        functools.partial(mix_kernel, n, seqs, rank, heads, dh),
        out_shape=(
            jax.ShapeDtypeStruct((rows, heads * dh), bf16),
            jax.ShapeDtypeStruct(head_output_weight.shape, bf16),
            jax.ShapeDtypeStruct(feedforward_weight.shape, bf16),
        ),
        in_specs=[smem, vmem, vmem, vmem, vmem, vmem, vmem, hbm, hbm, hbm, hbm],
        out_specs=(vmem, hbm, hbm),
        scratch_shapes=[
            pltpu.VMEM((2,) + query_key_value_weight.shape, bf16),
            pltpu.VMEM((width, 128), bf16),
            pltpu.VMEM((2, 128, head_cols), bf16),
            pltpu.VMEM((8, 128), jnp.float32),
            pltpu.VMEM((own * n, piece, dh), bf16),
            pltpu.VMEM((n, 8, 128), jnp.int32),
            pltpu.SMEM((n, 8, 128), jnp.int32),
            pltpu.VMEM((n, 2, seqs, piece, dh), bf16),
            pltpu.VMEM((2, n, seqs, piece, dh), bf16),
            pltpu.VMEM((rows, heads * dh), bf16),
            pltpu.VMEM((rows, heads * dh), bf16),
            pltpu.VMEM((rows, heads * dh), bf16),
            pltpu.VMEM((rows, heads * dh), jnp.float32),
            pltpu.VMEM((rows, heads * dh), jnp.float32),
            dma((n,)), dma((n,)), dma((n,)), dma((n,)), dma((2 * n,)), dma((2 * n,)), dma((6,)), dma((6,)), dma((5,)),
        ],
        compiler_params=pltpu.CompilerParams(
            collective_id=0, has_side_effects=True, vmem_limit_bytes=50 * 2**20),
        cost_estimate=pl.CostEstimate(flops=2 * 10**9, bytes_accessed=2 * 10**7, transcendentals=10**6),
    )(
        lengths.reshape(-1), index, tokens, norm_gain_pair, aux, up, bias, query_key_value_weight,
        caches.reshape(own, n, piece, dh), head_output_weight, feedforward_weight,
    )

    def by_owner(mine, theirs, axis):
        return (jnp.where(c == 0, mine, theirs), jnp.where(c == 0, theirs, mine))

    left, right = head_out[:, :head_cols], head_out[:, head_cols:]
    near, far = by_owner(left, right, 1)
    f32 = jnp.float32
    proj = jnp.dot(near, head_output_weight, preferred_element_type=f32) + jnp.dot(
        far, wo_other, preferred_element_type=f32)
    mixed = (tokens.astype(f32) + proj).astype(bf16)
    normed_two = rms_scale(mixed, norm_gain_pair[1])
    feed = mixed.astype(f32)
    for weight in (feedforward_weight, ff_other):
        gate_up = jnp.einsum("td,kdf->ktf", normed_two, weight[:2], preferred_element_type=f32)
        hidden = (jax.nn.silu(gate_up[0]) * gate_up[1]).astype(bf16)
        feed = feed + jnp.einsum("tf,df->td", hidden, weight[2], preferred_element_type=f32)
    return feed.astype(bf16)


def solution(mesh):
    placed = (
        P(("req", "col"), None),
        P(),
        P(None, None, "col"),
        P(None, None, "col"),
        P("col"),
        P("col", None, None),
        P(None, None, "col"),
        P("req", None, None),
        P("req", None),
        P("req", None),
        P("req", "col", None, None),
        P("col", None),
        P(None, None, "col"),
    )
    return jax.shard_map(
        on_device, mesh=mesh, in_specs=placed, out_specs=P(("req", "col"), None), check_vma=False
    )
```

time: 234 us -> 84.5 us (0.36)
  the two profiles are of different devices: /device:TPU:0 before, /device:TPU:29 now
where the time goes in v1:
time: 84.5 us; the launch traced here: 83.9 us
  Pallas kernels  43.1 us (51%)
  between operations  15.5 us (18%)
  matrix products  11.9 us (14%)
  local copies, waits for them, and re-layouts  8.4 us (10%)
  other arithmetic  4.92 us (6%)
    pallas_call x1, Pallas kernels, on_device(): pl.pallas_call(functools.partial(mix_kernel, n, seqs, rank, heads, dh), o...  43.1 us
    dot_general x2, matrix products, on_device(): jnp.einsum('td,kdf->ktf', normed_two, weight[:2], preferred_element_type=...  6.24 us
    dot_general x2, matrix products, on_device(): jnp.einsum('tf,df->td', hidden, weight[2], preferred_element_type=f32)  4.7 us
    select_n x4, other arithmetic, on_device(): jnp.where(held[s], lax.dynamic_index_in_dim(adapter_down_factor, jnp.clip...  3.91 us

profile of v1, /device:TPU:29, one launch (start us, length us, event | category | flops | bytes accessed | tf_op | source)
XLA Modules:
  0.0 83.9 jit_solution(6483602554111249352)
XLA Ops:
  0.0 0.8 reshape.149.lens_ref
  0.8 0.7 pad.8
  1.4 0.7 compare_and_fusion
  2.1 0.7 fusion.52
  6.6 0.9 %constant_dynamic-slice_fusion.3 = (bf16[1,1024,16]{1,2,0:T(8,128)(2,1)S(1)}, bf16[1,1024,16]{1,2,0:T(8,128)(2,1)S(1)}, bf16[1,1024,16]{1,2,0:T(8,128)(2,1)S(1)}...) fusion(bf16[32,1024,16]{1,2,0:T(8,128)(2,1)} %param.18, ...), kind=kLoop, calls=%fused_computation.59 | loop fusion | bytes 393240 | tf_op jit(solution)/shard_map/jit(dynamic_index_in_dim)/dynamic_slice | solution.py:262
  7.5 0.2 copy.40
  7.6 0.7 fusion.51
  8.3 0.6 select_bitcast_fusion.2
  9.0 0.2 copy.42
  9.2 0.2 copy.41
  9.3 1.3 %select_bitcast_fusion = (bf16[1024,16]{1,0:T(8,128)(2,1)S(1)}, bf16[1024,16]{1,0:T(8,128)(2,1)S(1)}) fusion(bf16[1,1024,16]{2,1,0:T(8,128)(2,1)S(1)} %copy.42, pred[]{:T(512)} %bitcast.17, bf16[1,1024,16]{2,1,0:T(8,128)(2,1)S(1)} %copy.41, pred[]{:T(512)} %bitcast.14), kind=kLoop, calls=%fused_computation.35 | loop fusion | flops 32768 | bytes 131074 | tf_op jit(solution)/shard_map/jit(_where)/select_n | solution.py:262
  10.7 0.1 broadcast_select_fusion
  10.8 0.2 copy.26
  11.0 0.2 copy.27
  11.2 0.7 concatenate.13
  12.0 0.2 copy.37
  12.1 0.6 select_bitcast_fusion.5
  12.8 0.2 copy.39
  13.0 0.2 copy.38
  13.1 1.4 %select_bitcast_fusion.3 = (bf16[1024,16]{1,0:T(8,128)(2,1)S(1)}, bf16[1024,16]{1,0:T(8,128)(2,1)S(1)}) fusion(bf16[1,1024,16]{2,1,0:T(8,128)(2,1)S(1)} %copy.39, pred[]{:T(512)} %bitcast.7, bf16[1,1024,16]{2,1,0:T(8,128)(2,1)S(1)} %copy.38, pred[]{:T(512)} %bitcast.4), kind=kLoop, calls=%fused_computation.38 | loop fusion | flops 32768 | bytes 131074 | tf_op jit(solution)/shard_map/jit(_where)/select_n | solution.py:262
  14.5 0.7 concatenate.12
  15.3 0.7 fusion.50
  27.4 0.8 dynamic-slice_bitcast_fusion.5
  28.3 0.1 maximum_bitcast_fusion
  28.5 0.1 select_n.133
  28.7 43.1 %shard_map.127 = (bf16[256,1024]{1,0:T(8,128)(2,1)S(1)}, bf16[512,1024]{1,0:T(8,128)(2,1)S(1)}, bf16[3,1024,1408]{2,1,0:T(8,128)(2,1)}) custom-call(s32[6]{0:T(128)S(1)} %reshape.149.lens_ref, s32[8,128]{1,0:T(8,128)S(1)} %broadcast_in_dim.71.idx_ref, bf16[256,1024]{1,0:T(8,128)(2,1)S(1)} %copy-done, f32[2,1024]{1,0:T(2,128)S(1)} %copy-done.2, ...), custom_call_target="tpu_custom_call" | custom-call | flops 2000000000 | bytes 20000000 | tf_op jit(solution)/shard_map/pallas_call | solution.py:284
  71.8 0.4 fusion.39
  72.3 0.6 fusion.28
  72.9 4.5 %fusion.4 = f32[2,256,1408]{2,1,0:T(8,128)S(1)} fusion(bf16[3,1024,1408]{2,1,0:T(8,128)(2,1)} %ff_ref.1, bf16[256,1024]{1,0:T(8,128)(2,1)S(1)} %get-tuple-element.48, f32[1024]{0:T(1024)S(1)} %bitcast.86, f32[256]{0:T(256)S(1)} %add_rsqrt_fusion), kind=kOutput, calls=%fused_computation.4 | convolution fusion | flops 1477443584 | bytes 9180160 | tf_op jit(solution)/shard_map/td,kdf->ktf/dot_general | solution.py:330
  77.4 2.9 %convert_add_fusion = f32[256,1024]{1,0:T(8,128)S(1)} fusion(bf16[256,1024]{1,0:T(8,128)(2,1)S(1)} %get-tuple-element.48, bf16[3,1024,1408]{2,1,0:T(8,128)(2,1)} %ff_ref.1, f32[2,256,1408]{2,1,0:T(8,128)S(1)} %fusion.4), kind=kOutput, calls=%fused_computation.12 | convolution fusion | flops 740884480 | bytes 7340032 | tf_op jit(solution)/shard_map/tf,df->td/dot_general | solution.py:332
  80.3 1.7 %fusion.7 = f32[2,256,1408]{2,1,0:T(8,128)S(1)} fusion(bf16[3,1024,1408]{2,1,0:T(8,128)(2,1)S(1)} %bitcast.89, bf16[256,1024]{1,0:T(8,128)(2,1)S(1)} %get-tuple-element.48, f32[1024]{0:T(1024)S(1)} %bitcast.87, f32[256]{0:T(256)S(1)} %add_rsqrt_fusion), kind=kOutput, calls=%fused_computation.5 | convolution fusion | flops 1477443584 | bytes 9180160 | tf_op jit(solution)/shard_map/td,kdf->ktf/dot_general | solution.py:330
  82.1 1.8 %fusion.24 = bf16[256,1024]{1,0:T(8,128)(2,1)} fusion(f32[256,1024]{1,0:T(8,128)S(1)} %convert_add_fusion, bf16[3,1024,1408]{2,1,0:T(8,128)(2,1)S(1)} %bitcast.89, f32[2,256,1408]{2,1,0:T(8,128)S(1)} %fusion.7), kind=kOutput, calls=%fused_computation.22 | convolution fusion | flops 740884480 | bytes 7340032 | tf_op jit(solution)/shard_map/tf,df->td/dot_general | solution.py:332
  (36 shorter events, 0.5 us)
Async XLA Ops:
  0.0 10.7 %copy-start.5 = (bf16[2,1024,4]{1,2,0:T(4,128)(2,1)S(1)}, bf16[2,1024,4]{1,2,0:T(4,128)(2,1)}, u32[]{:S(2)}) copy-start(bf16[2,1024,4]{1,2,0:T(4,128)(2,1)} %param.16) | copy-start | bytes 49156
  12.0 3.4 %copy-start.4 = (s32[1,6]{1,0:T(1,128)S(1)}, s32[1,6]{1,0:T(1,128)}, u32[]{:S(2)}) copy-start(s32[1,6]{1,0:T(1,128)} %param.21) | copy-start | bytes 76
  12.7 15.7 %copy-start.6 = (f32[4]{0:T(128)S(1)}, f32[4]{0:T(128)}, u32[]{:S(2)}) copy-start(f32[4]{0:T(128)} %param.17) | copy-start | bytes 52
  12.8 15.9 %copy-start = (bf16[256,1024]{1,0:T(8,128)(2,1)S(1)}, bf16[256,1024]{1,0:T(8,128)(2,1)}, u32[]{:S(2)}) copy-start(bf16[256,1024]{1,0:T(8,128)(2,1)} %tok_ref.1) | copy-start | bytes 1572868
  12.8 15.9 %copy-start.1 = (bf16[4,4,128,128]{3,2,1,0:T(8,128)(2,1)S(1)}, bf16[4,4,128,128]{3,2,1,0:T(8,128)(2,1)}, u32[]{:S(2)}) copy-start(bf16[4,4,128,128]{3,2,1,0:T(8,128)(2,1)} %param.23) | copy-start | bytes 1572868
  12.8 15.9 %copy-start.2 = (f32[2,1024]{1,0:T(2,128)S(1)}, f32[2,1024]{1,0:T(2,128)}, u32[]{:S(2)}) copy-start(f32[2,1024]{1,0:T(2,128)} %gain_ref.1) | copy-start | bytes 24580
  28.7 43.2 %copy-start.3 = (bf16[512,1024]{1,0:T(8,128)(2,1)S(1)}, bf16[512,1024]{1,0:T(8,128)(2,1)}, u32[]{:S(2)}) copy-start(bf16[512,1024]{1,0:T(8,128)(2,1)} %wo_ref.1) | copy-start | bytes 3145732
  72.9 7.4 %slice-start = ((s8[8650752]{0:T(1024)(128)(4,1)}), s8[4194304]{0:T(1024)(128)(4,1)S(1)}, s32[]{:S(2)}) async-start(s8[8650752]{0:T(1024)(128)(4,1)} %bitcast.88), calls=%async_computation | async-start | bytes 8388608
  72.9 7.4 %slice-start.1 = ((s8[8650752]{0:T(1024)(128)(4,1)}), s8[4194304]{0:T(1024)(128)(4,1)S(1)}, s32[]{:S(2)}) async-start(s8[8650752]{0:T(1024)(128)(4,1)} %bitcast.88), calls=%async_computation.1 | async-start | bytes 8388608
  77.4 2.9 %slice-start.2 = ((s8[8650752]{0:T(1024)(128)(4,1)}), s8[262144]{0:T(1024)(128)(4,1)S(1)}, s32[]{:S(2)}) async-start(s8[8650752]{0:T(1024)(128)(4,1)} %bitcast.88), calls=%async_computation.2 | async-start | bytes 524288

commit v2 on v1

v2 whole, which is shorter than its diff:
```python
import functools
import math

import jax
import jax.numpy as jnp
from jax import lax
from jax.experimental import pallas as pl
from jax.experimental.pallas import tpu as pltpu
from jax.sharding import PartitionSpec as P

epsilon = 1e-05
MESH = pl.DeviceIdType.MESH


def mix_kernel(
    n, seqs, rank, half, dh,
    lens_ref, aidx_ref, cidx_ref, bias_ref, tok_ref, gain_ref, gate_ref, down_ref, up_ref,
    qkv_ref, cache_ref, wo_ref, ff_ref,
    out_ref,
    down_v, up_v, aux_s, auxr, upsel, upr, biasr, gates, wq, wo, wff, r1, idxb, idxs, stage, r2,
    q_s, k_s, v_s, att_s, intra_s, head_s,
    s1, t1, si, ti, s2, t2, sp, tp, lsem,
):
    g = lax.axis_index("req")
    c = lax.axis_index("col")
    other = 1 - c
    me = g * 2 + c
    total = n * 2
    own = cache_ref.shape[0]
    rows = tok_ref.shape[0]
    adapters = down_ref.shape[0]
    base = seqs * rank
    f32, bf16 = jnp.float32, jnp.bfloat16

    barrier = pltpu.get_barrier_semaphore()

    def greet(k, carry):
        d = lax.rem(me + k, total)
        pl.semaphore_signal(barrier, inc=1, device_id=(d // 2, lax.rem(d, 2)), device_id_type=MESH)
        return carry

    lax.fori_loop(1, total, greet, 0)

    def local(src, dst, i):
        one = pltpu.make_async_copy(src, dst, lsem.at[i])
        one.start()
        return one

    local_down = local(down_ref, down_v, 0)
    local_up = local(up_ref, up_v, 1)
    local_c = local(cache_ref.at[:, g], r1.at[pl.ds(own * g, own)], 2)
    local_w = local(qkv_ref, wq.at[0], 3)
    local_wo = local(wo_ref, wo.at[0], 4)
    local_ff = local(ff_ref, wff.at[0], 5)

    lane8 = lax.broadcasted_iota(jnp.int32, (8, 128), 1)
    index = jnp.zeros((8, 128), jnp.int32)
    for s in range(2 * seqs):
        index = jnp.where(lane8 == s, cidx_ref[0, s], index)
    idxb[g] = index
    bias = jnp.zeros((8, 128), f32)
    for h in range(half):
        bias = jnp.where(lane8 == h, bias_ref[h], bias)
    biasr[0] = bias
    gates[0] = gate_ref[...]

    pl.semaphore_wait(barrier, total - 1)

    def cache_copy(p, slot):
        return pltpu.make_async_remote_copy(
            src_ref=cache_ref.at[:, p], dst_ref=r1.at[pl.ds(own * slot, own)],
            send_sem=s1.at[p], recv_sem=t1.at[slot], device_id=(p, c), device_id_type=MESH)

    def index_copy(p, slot):
        return pltpu.make_async_remote_copy(
            src_ref=idxb.at[g], dst_ref=idxb.at[slot],
            send_sem=si.at[p], recv_sem=ti.at[slot], device_id=(p, c), device_id_type=MESH)

    def first(k, carry):
        p = lax.rem(g + k, n)
        index_copy(p, g).start()
        cache_copy(p, g).start()
        return carry

    lax.fori_loop(1, n, first, 0)

    pairs = []

    def pair(src, dst):
        i = len(pairs)
        one = pltpu.make_async_remote_copy(
            src_ref=src, dst_ref=dst, send_sem=sp.at[i], recv_sem=tp.at[i],
            device_id=(g, other), device_id_type=MESH)
        one.start()
        pairs.append(one)
        return one

    pair_gates = pair(gates.at[0], gates.at[1])
    pair_bias = pair(biasr.at[0], biasr.at[1])

    local_down.wait()
    local_up.wait()
    for b in range(2):
        for j in range(seqs):
            a = aidx_ref[0, b * seqs + j]
            mine_at = a - c * adapters
            held = (mine_at >= 0) & (mine_at < adapters)
            factor = down_v[jnp.clip(mine_at, 0, adapters - 1)]
            aux_s[b, j * rank:(j + 1) * rank, :] = jnp.where(held, factor, jnp.zeros_like(factor))
            upsel[b, j * rank:(j + 1) * rank, :] = up_v[a]
    pair_aux = pair(aux_s.at[other], auxr)
    pair_up = pair(upsel.at[other], upr)
    pair_w = pair(qkv_ref, wq.at[1])
    pair_wo = pair(wo_ref, wo.at[1])
    pair_ff = [pair(ff_ref.at[k], wff.at[1, k]) for k in range(3)]

    x = tok_ref[...].astype(f32)
    factor = lax.rsqrt(jnp.mean(x * x, axis=-1, keepdims=True) + epsilon)
    normed = (x * factor * gain_ref[0:1, :]).astype(bf16)

    ends = [lens_ref[0, c, 0]]
    for j in range(1, seqs - 1):
        ends.append(ends[-1] + lens_ref[0, c, j])

    def segment_of(shape, axis):
        pos = lax.broadcasted_iota(jnp.int32, shape, axis)
        seg = jnp.zeros(shape, jnp.int32)
        for e in ends:
            seg = seg + (pos >= e).astype(jnp.int32)
        return pos, seg

    q_pos, q_seg = segment_of((rows, rows), 0)
    k_pos, k_seg = segment_of((rows, rows), 1)
    allowed = (q_seg == k_seg) & (k_pos <= q_pos)
    _, seg_wide = segment_of((rows, 128), 0)
    _, seg_low = segment_of((rows, base), 0)

    local_w.wait()
    width = half * dh
    cols = pl.ds(0, width)
    own_q = jnp.dot(normed, wq[0, 0], preferred_element_type=f32)
    k_s[:, cols] = jnp.dot(normed, wq[0, 1], preferred_element_type=f32).astype(bf16)
    v_s[:, cols] = jnp.dot(normed, wq[0, 2], preferred_element_type=f32).astype(bf16)

    pair_gates.wait_recv()
    pair_bias.wait_recv()
    pair_aux.wait_recv()
    pair_up.wait_recv()
    nt = (((1,), (1,)), ((), ()))
    down = aux_s[c] + auxr[...]
    low = lax.dot_general(normed, down, nt, preferred_element_type=f32)
    lane = lax.broadcasted_iota(jnp.int32, (rows, base), 1)
    low = jnp.where(lane // rank == seg_low, low, 0.0).astype(bf16)
    own_q = own_q + jnp.dot(low, upsel[c], preferred_element_type=f32)
    q_s[:, cols] = own_q.astype(bf16)

    ones = allowed.astype(f32).astype(bf16)
    levels, levels_t, mixes = [], [], []
    for b in range(2):
        terms = lax.dot_general(normed, gates[b], nt, preferred_element_type=f32)
        shifted = terms + biasr[b][0:1, :]
        log_keep = jnp.minimum(shifted, 0.0) - jnp.log1p(jnp.exp(-jnp.abs(shifted)))
        mixes.append(1.0 / (1.0 + jnp.exp(-terms)))
        part = log_keep.astype(bf16)
        level = jnp.dot(ones, part, preferred_element_type=f32)
        rest = log_keep - part.astype(f32)
        part = rest.astype(bf16)
        level = level + jnp.dot(ones, part, preferred_element_type=f32)
        part = (rest - part.astype(f32)).astype(bf16)
        level = level + jnp.dot(ones, part, preferred_element_type=f32)
        levels.append(level)
        levels_t.append(jnp.transpose(level))

    local_c.wait()

    def first_wait(k, carry):
        p = lax.rem(g + k, n)
        index_copy(p, p).wait_recv()
        cache_copy(p, p).wait_recv()
        return carry

    lax.fori_loop(1, n, first_wait, 0)
    local(idxb, idxs, 6).wait()

    def pick(p):
        for b in range(2):
            for j in range(seqs):
                i = idxs[p, 0, b * seqs + j]
                piece = r1[jnp.minimum(i, own * n - 1)]
                stage[p, b, j] = jnp.where(i < own * n, piece, jnp.zeros_like(piece))

    def second_copy(d, slot_c, slot_g):
        return pltpu.make_async_remote_copy(
            src_ref=stage.at[d // 2, lax.rem(d, 2)], dst_ref=r2.at[slot_c, slot_g],
            send_sem=s2.at[d], recv_sem=t2.at[slot_c * n + slot_g],
            device_id=(d // 2, lax.rem(d, 2)), device_id_type=MESH)

    def second(k, carry):
        p = lax.rem(g + k, n)
        pick(p)
        second_copy(p * 2 + c, 0, g).start()
        second_copy(p * 2 + other, 1, g).start()
        return carry

    lax.fori_loop(1, n, second, 0)
    pick(g)
    second_copy(g * 2 + other, 1, g).start()
    keep = local(stage.at[g, c], r2.at[0, g], 7)

    scale = 1.0 / math.sqrt(dh)

    def attend(h):
        cols = pl.ds(h * dh, dh)
        b, i = h // half, h % half
        scores = lax.dot_general(q_s[:, cols], k_s[:, cols], nt, preferred_element_type=f32) * scale
        masked = jnp.where(allowed, scores, -jnp.inf)
        peak = jnp.max(masked, axis=1, keepdims=True)
        weights = jnp.exp(masked - peak)
        probs = (weights / jnp.sum(weights, axis=1, keepdims=True)).astype(bf16)
        att_s[:, cols] = jnp.dot(probs, v_s[:, cols], preferred_element_type=f32)
        gap = jnp.where(allowed, levels[b][:, i:i + 1] - levels_t[b][i:i + 1, :], -jnp.inf)
        memory_w = (scores * jnp.exp(gap)).astype(bf16)
        intra_s[:, cols] = jnp.dot(memory_w, v_s[:, cols], preferred_element_type=f32)

    for h in range(half):
        attend(h)
    pair_w.wait_recv()
    cols = pl.ds(width, width)
    q = jnp.dot(normed, wq[1, 0], preferred_element_type=f32)
    q_s[:, cols] = (q + jnp.dot(low, upr[...], preferred_element_type=f32)).astype(bf16)
    k_s[:, cols] = jnp.dot(normed, wq[1, 1], preferred_element_type=f32).astype(bf16)
    v_s[:, cols] = jnp.dot(normed, wq[1, 2], preferred_element_type=f32).astype(bf16)
    for h in range(half, 2 * half):
        attend(h)

    keep.wait()

    def second_wait(k, carry):
        p = lax.rem(g + k, n)
        second_copy(p * 2 + c, 0, p).wait_recv()
        second_copy(p * 2 + other, 1, p).wait_recv()
        return carry

    lax.fori_loop(1, n, second_wait, 0)
    second_copy(g * 2 + other, 1, g).wait_recv()

    per_head = n // half
    for h in range(2 * half):
        cols = pl.ds(h * dh, dh)
        b, i = h // half, h % half
        q = q_s[:, cols]
        carried = jnp.zeros((rows, dh), f32)
        for j in range(seqs):
            state = r2[b, i * per_head:(i + 1) * per_head, j]
            state = state.astype(f32).reshape(dh, dh).astype(bf16)
            carried = jnp.where(seg_wide == j, jnp.dot(q, state, preferred_element_type=f32), carried)
        recalled = carried * jnp.exp(levels[b][:, i:i + 1]) + intra_s[:, cols]
        factor = lax.rsqrt(jnp.mean(recalled * recalled, axis=1, keepdims=True) + epsilon)
        head_s[:, cols] = (att_s[:, cols] + mixes[b][:, half + i:half + i + 1] * recalled * factor).astype(bf16)

    local_wo.wait()
    pair_wo.wait_recv()
    proj = jnp.dot(head_s[:, :width], wo[0], preferred_element_type=f32)
    proj = proj + jnp.dot(head_s[:, width:], wo[1], preferred_element_type=f32)
    mixed = (tok_ref[...].astype(f32) + proj).astype(bf16).astype(f32)
    factor = lax.rsqrt(jnp.mean(mixed * mixed, axis=-1, keepdims=True) + epsilon)
    normed_two = (mixed * factor * gain_ref[1:2, :]).astype(bf16)
    feed = mixed
    local_ff.wait()
    for b in range(2):
        if b == 1:
            pair_ff[0].wait_recv()
        gate = jnp.dot(normed_two, wff[b, 0], preferred_element_type=f32)
        if b == 1:
            pair_ff[1].wait_recv()
        upper = jnp.dot(normed_two, wff[b, 1], preferred_element_type=f32)
        hidden = (gate / (1.0 + jnp.exp(-gate)) * upper).astype(bf16)
        if b == 1:
            pair_ff[2].wait_recv()
        feed = feed + lax.dot_general(hidden, wff[b, 2], nt, preferred_element_type=f32)
    out_ref[...] = feed.astype(bf16)

    def drain(k, carry):
        p = lax.rem(g + k, n)
        index_copy(p, g).wait_send()
        cache_copy(p, g).wait_send()
        second_copy(p * 2 + c, 0, g).wait_send()
        second_copy(p * 2 + other, 1, g).wait_send()
        return carry

    lax.fori_loop(1, n, drain, 0)
    second_copy(g * 2 + other, 1, g).wait_send()
    for one in pairs:
        one.wait_send()


def on_device(
    tokens, norm_gain_pair, query_key_value_weight, head_gate_weight, decay_logit_bias,
    adapter_down_factor, adapter_up_factor, lengths, request_adapter_index, request_cache_index,
    caches, head_output_weight, feedforward_weight,
):
    n = lax.axis_size("req")
    rows, width = tokens.shape
    seqs = lengths.shape[2]
    adapters, _, rank = adapter_down_factor.shape
    half = head_gate_weight.shape[2]
    head_cols = query_key_value_weight.shape[2]
    dh = head_cols // half
    own = caches.shape[0]
    piece = half * dh // n
    base = seqs * rank
    bf16, f32 = jnp.bfloat16, jnp.float32

    gate = head_gate_weight.transpose(0, 2, 1).reshape(2 * half, width)
    gate = jnp.pad(gate, ((0, 128 - 2 * half), (0, 0)))

    vmem = pl.BlockSpec(memory_space=pltpu.VMEM)
    smem = pl.BlockSpec(memory_space=pltpu.SMEM)
    hbm = pl.BlockSpec(memory_space=pl.ANY)
    dma = pltpu.SemaphoreType.DMA
    wide = 2 * head_cols
    return pl.pallas_call(
        functools.partial(mix_kernel, n, seqs, rank, half, dh),
        out_shape=jax.ShapeDtypeStruct((rows, width), bf16),
        in_specs=[smem] * 4 + [vmem] * 3 + [hbm] * 6,
        out_specs=vmem,
        scratch_shapes=[
            pltpu.VMEM((adapters, rank, width), bf16),
            pltpu.VMEM(adapter_up_factor.shape, bf16),
            pltpu.VMEM((2, base, width), bf16),
            pltpu.VMEM((base, width), bf16),
            pltpu.VMEM((2, base, head_cols), bf16),
            pltpu.VMEM((base, head_cols), bf16),
            pltpu.VMEM((2, 8, 128), f32),
            pltpu.VMEM((2, 128, width), bf16),
            pltpu.VMEM((2,) + query_key_value_weight.shape, bf16),
            pltpu.VMEM((2,) + head_output_weight.shape, bf16),
            pltpu.VMEM((2,) + feedforward_weight.shape, bf16),
            pltpu.VMEM((own * n, piece, dh), bf16),
            pltpu.VMEM((n, 8, 128), jnp.int32),
            pltpu.SMEM((n, 8, 128), jnp.int32),
            pltpu.VMEM((n, 2, seqs, piece, dh), bf16),
            pltpu.VMEM((2, n, seqs, piece, dh), bf16),
            pltpu.VMEM((rows, wide), bf16),
            pltpu.VMEM((rows, wide), bf16),
            pltpu.VMEM((rows, wide), bf16),
            pltpu.VMEM((rows, wide), f32),
            pltpu.VMEM((rows, wide), f32),
            pltpu.VMEM((rows, wide), bf16),
            dma((n,)), dma((n,)), dma((n,)), dma((n,)), dma((2 * n,)), dma((2 * n,)),
            dma((10,)), dma((10,)), dma((8,)),
        ],
        compiler_params=pltpu.CompilerParams(
            collective_id=0, has_side_effects=True, vmem_limit_bytes=56 * 2**20),
        cost_estimate=pl.CostEstimate(flops=7 * 10**9, bytes_accessed=3 * 10**7, transcendentals=10**6),
    )(
        lengths, request_adapter_index, request_cache_index, decay_logit_bias, tokens, norm_gain_pair,
        gate, adapter_down_factor.transpose(0, 2, 1), adapter_up_factor, query_key_value_weight,
        caches.reshape(own, n, piece, dh), head_output_weight, feedforward_weight,
    )


def solution(mesh):
    placed = (
        P(("req", "col"), None),
        P(),
        P(None, None, "col"),
        P(None, None, "col"),
        P("col"),
        P("col", None, None),
        P(None, None, "col"),
        P("req", None, None),
        P("req", None),
        P("req", None),
        P("req", "col", None, None),
        P("col", None),
        P(None, None, "col"),
    )
    return jax.shard_map(
        on_device, mesh=mesh, in_specs=placed, out_specs=P(("req", "col"), None), check_vma=False
    )
```

time: 84.5 us -> 53.9 us (0.64)
  between operations: 15.5 us -> 0.01 us
  matrix products: 11.9 us -> 0 us
  Pallas kernels: 43.1 us -> 50.3 us
  local copies, waits for them, and re-layouts: 8.4 us -> 3.33 us
  other arithmetic: 4.92 us -> 0 us
    dot_general x6 -> x0, matrix products: 11.9 us -> none  [the longest x2 6.24 us: on_device(): jnp.einsum('td,kdf->ktf', normed_two, weight[:2], preferred_element_type=...]
    pallas_call x1, Pallas kernels: 43.1 us -> 50.3 us  [on_device(): pl.pallas_call(functools.partial(mix_kernel, n, seqs, rank, half, dh), ou...]
    select_n x6 -> x0, other arithmetic: 4.07 us -> none  [the longest x4 3.91 us: on_device(): jnp.where(held[s], lax.dynamic_index_in_dim(adapter_down_factor, jnp.clip...]
    slice x5 -> x0, local copies, waits for them, and re-layouts: 2.06 us -> none  [the longest x1 0.69 us: on_device(): held[s]]
    concatenate x3 -> x0, local copies, waits for them, and re-layouts: 1.54 us -> none  [the longest x2 1.46 us: on_device(): jnp.concatenate(picked[b * seqs:(b + 1) * seqs] + [gates[0], gates[1], fi...]
    squeeze x5 -> x0, local copies, waits for them, and re-layouts: 1.19 us -> none  [the longest x1 0.82 us: on_device(): lax.dynamic_index_in_dim(adapter_up_factor, which[s], 0, keepdims=False)]
    dynamic_slice x1 -> x0, local copies, waits for them, and re-layouts: 0.9 us -> none  [on_device(): lax.dynamic_index_in_dim(adapter_down_factor, jnp.clip(local[s], 0, adapt...]
    unnamed x26 -> x1, local copies, waits for them, and re-layouts: 1.08 us -> 1.87 us
where the time goes in v2:
time: 53.9 us; the launch traced here: 53.7 us
  Pallas kernels  50.3 us (93%)
  local copies, waits for them, and re-layouts  3.33 us (6%)
    pallas_call x1, Pallas kernels, on_device(): pl.pallas_call(functools.partial(mix_kernel, n, seqs, rank, half, dh), ou...  50.3 us
    unnamed x1, local copies, waits for them, and re-layouts  1.87 us

profile of v2, /device:TPU:29, one launch (start us, length us, event | category | flops | bytes accessed | tf_op | source)
XLA Modules:
  0.0 53.7 jit_solution(2538030723557618487)
XLA Ops:
  0.0 0.7 %reshape.6 = bf16[8,1024]{1,0:T(8,128)(2,1)S(1)} reshape(bf16[2,4,1024]{2,1,0:T(4,128)(2,1)} %bitcast.3) | data formatting | bytes 32768 | tf_op jit(solution)/shard_map/reshape | solution.py:314
  0.7 0.7 %pad.4.gate_ref = bf16[128,1024]{1,0:T(8,128)(2,1)} pad(bf16[8,1024]{1,0:T(8,128)(2,1)S(1)} %reshape.6, bf16[]{:T(256)} %constant.2.clone.1), padding=0_120x0_0 | pad | bytes 278530 | tf_op jit(solution)/shard_map/jit(_pad)/pad | solution.py:315
  1.5 50.3 %shard_map.127 = bf16[256,1024]{1,0:T(8,128)(2,1)} custom-call(s32[1,2,3]{2,1,0:T(2,128)} %lens_ref.1, s32[1,6]{1,0:T(1,128)} %aidx_ref.1, s32[1,6]{1,0:T(1,128)} %cidx_ref.1, f32[4]{0:T(128)} %bias_ref.1, bf16[256,1024]{1,0:T(8,128)(2,1)} %tok_ref.1, f32[2,1024]{1,0:T(2,128)} %gain_ref.1, bf16[128,1024]{1,0:T(8,128)(2,1)} %pad.4.gate_ref, ...), custom_call_target="tpu_custom_call" | custom-call | flops 7000000000 | bytes 30000000 | tf_op jit(solution)/shard_map/pallas_call | solution.py:322
  51.8 1.9 %copy.15 = bf16[256,1024]{1,0:T(8,128)(2,1)} copy(bf16[256,1024]{1,0:T(8,128)(2,1)} %shard_map.127) | data formatting | bytes 1048576

commit v3 on v2

--- a/solution.py
+++ b/solution.py
@@ -62,7 +62,8 @@
     for h in range(half):
         bias = jnp.where(lane8 == h, bias_ref[h], bias)
     biasr[0] = bias
-    gates[0] = gate_ref[...]
+    zeros = jnp.zeros((128 - 2 * half, gate_ref.shape[2]), f32)
+    gates[0] = jnp.concatenate([gate_ref[0].astype(f32), gate_ref[1].astype(f32), zeros], axis=0).astype(bf16)
 
     pl.semaphore_wait(barrier, total - 1)
 
@@ -112,7 +113,7 @@
     pair_up = pair(upsel.at[other], upr)
     pair_w = pair(qkv_ref, wq.at[1])
     pair_wo = pair(wo_ref, wo.at[1])
-    pair_ff = [pair(ff_ref.at[k], wff.at[1, k]) for k in range(3)]
+    pair_ff = [pair(ff_ref.at[0], wff.at[1, 0])]
 
     x = tok_ref[...].astype(f32)
     factor = lax.rsqrt(jnp.mean(x * x, axis=-1, keepdims=True) + epsilon)
@@ -206,6 +207,7 @@
     pick(g)
     second_copy(g * 2 + other, 1, g).start()
     keep = local(stage.at[g, c], r2.at[0, g], 7)
+    pair_ff += [pair(ff_ref.at[k], wff.at[1, k]) for k in range(1, 3)]
 
     scale = 1.0 / math.sqrt(dh)
 
@@ -278,7 +280,7 @@
         if b == 1:
             pair_ff[2].wait_recv()
         feed = feed + lax.dot_general(hidden, wff[b, 2], nt, preferred_element_type=f32)
-    out_ref[...] = feed.astype(bf16)
+    out_ref[...] = feed
 
     def drain(k, carry):
         p = lax.rem(g + k, n)
@@ -311,17 +313,14 @@
     base = seqs * rank
     bf16, f32 = jnp.bfloat16, jnp.float32
 
-    gate = head_gate_weight.transpose(0, 2, 1).reshape(2 * half, width)
-    gate = jnp.pad(gate, ((0, 128 - 2 * half), (0, 0)))
-
     vmem = pl.BlockSpec(memory_space=pltpu.VMEM)
     smem = pl.BlockSpec(memory_space=pltpu.SMEM)
     hbm = pl.BlockSpec(memory_space=pl.ANY)
     dma = pltpu.SemaphoreType.DMA
     wide = 2 * head_cols
-    return pl.pallas_call(
+    layer = pl.pallas_call(
         functools.partial(mix_kernel, n, seqs, rank, half, dh),
-        out_shape=jax.ShapeDtypeStruct((rows, width), bf16),
+        out_shape=jax.ShapeDtypeStruct((rows, width), f32),
         in_specs=[smem] * 4 + [vmem] * 3 + [hbm] * 6,
         out_specs=vmem,
         scratch_shapes=[
@@ -355,9 +354,10 @@
         cost_estimate=pl.CostEstimate(flops=7 * 10**9, bytes_accessed=3 * 10**7, transcendentals=10**6),
     )(
         lengths, request_adapter_index, request_cache_index, decay_logit_bias, tokens, norm_gain_pair,
-        gate, adapter_down_factor.transpose(0, 2, 1), adapter_up_factor, query_key_value_weight,
+        head_gate_weight.transpose(0, 2, 1), adapter_down_factor.transpose(0, 2, 1), adapter_up_factor, query_key_value_weight,
         caches.reshape(own, n, piece, dh), head_output_weight, feedforward_weight,
     )
+    return layer.astype(bf16)
 
 
 def solution(mesh):

time: 53.9 us -> 52.8 us (0.980)
  local copies, waits for them, and re-layouts: 3.33 us -> 0 us
  other arithmetic: 0 us -> 2.1 us
    convert_element_type x0 -> x1, other arithmetic: none -> 2.1 us  [on_device(): return layer.astype(bf16)]
    unnamed x1 -> x0, local copies, waits for them, and re-layouts: 1.87 us -> none
    pad x1 -> x0, local copies, waits for them, and re-layouts: 0.73 us -> none  [on_device(): gate = jnp.pad(gate, ((0, 128 - 2 * half), (0, 0)))]
    reshape x1 -> x0, local copies, waits for them, and re-layouts: 0.73 us -> none  [on_device(): gate = head_gate_weight.transpose(0, 2, 1).reshape(2 * half, width)]
where the time goes in v3:
time: 52.8 us; the launch traced here: 52.6 us
  Pallas kernels  50.5 us (96%)
  other arithmetic  2.1 us (4%)
    pallas_call x1, Pallas kernels, on_device(): pl.pallas_call(functools.partial(mix_kernel, n, seqs, rank, half, dh), ou...  50.5 us
    convert_element_type x1, other arithmetic, on_device(): return layer.astype(bf16)  2.1 us

profile of v3, /device:TPU:29, one launch (start us, length us, event | category | flops | bytes accessed | tf_op | source)
XLA Modules:
  0.0 52.6 jit_solution(10129795858956384915)
XLA Ops:
  0.0 50.5 %shard_map.127 = f32[256,1024]{1,0:T(8,128)} custom-call(s32[1,2,3]{2,1,0:T(2,128)} %lens_ref.1, s32[1,6]{1,0:T(1,128)} %aidx_ref.1, s32[1,6]{1,0:T(1,128)} %cidx_ref.1, f32[4]{0:T(128)} %bias_ref.1, bf16[256,1024]{1,0:T(8,128)(2,1)} %tok_ref.1, f32[2,1024]{1,0:T(2,128)} %gain_ref.1, bf16[2,4,1024]{2,1,0:T(4,128)(2,1)} %bitcast.5, ...), custom_call_target="tpu_custom_call" | custom-call | flops 7000000000 | bytes 30000000 | tf_op jit(solution)/shard_map/pallas_call | solution.py:321
  50.5 2.1 %convert_element_type.3 = bf16[256,1024]{1,0:T(8,128)(2,1)} convert(f32[256,1024]{1,0:T(8,128)} %shard_map.127) | non-fusion elementwise | flops 262144 | bytes 1572864 | tf_op jit(solution)/shard_map/convert_element_type | solution.py:360

commit v4 on v2

--- a/solution.py
+++ b/solution.py
@@ -17,15 +17,17 @@
     lens_ref, aidx_ref, cidx_ref, bias_ref, tok_ref, gain_ref, gate_ref, down_ref, up_ref,
     qkv_ref, cache_ref, wo_ref, ff_ref,
     out_ref,
-    down_v, up_v, aux_s, auxr, upsel, upr, biasr, gates, wq, wo, wff, r1, idxb, idxs, stage, r2,
+    down_v, up_v, aux_s, auxr, upsel, upr, biasr, gates, wq, wo, wff, r1_0, r1_1, idxb, idxs, stage, r2,
     q_s, k_s, v_s, att_s, intra_s, head_s,
     s1, t1, si, ti, s2, t2, sp, tp, lsem,
 ):
     g = lax.axis_index("req")
     c = lax.axis_index("col")
     other = 1 - c
-    me = g * 2 + c
-    total = n * 2
+    r1 = (r1_0, r1_1)
+    nh = n // 2
+    start = (g // nh) * nh
+    place = g - start
     own = cache_ref.shape[0]
     rows = tok_ref.shape[0]
     adapters = down_ref.shape[0]
@@ -34,12 +36,19 @@
 
     barrier = pltpu.get_barrier_semaphore()
 
+    def hello(p, core):
+        pl.semaphore_signal(barrier, inc=1, device_id=(p, core), device_id_type=MESH)
+
     def greet(k, carry):
-        d = lax.rem(me + k, total)
-        pl.semaphore_signal(barrier, inc=1, device_id=(d // 2, lax.rem(d, 2)), device_id_type=MESH)
-        return carry
-
-    lax.fori_loop(1, total, greet, 0)
+        hello(lax.rem(g + k, n), c)
+        return carry
+
+    def greet_half(k, carry):
+        hello(start + k, other)
+        return carry
+
+    lax.fori_loop(1, n, greet, 0)
+    lax.fori_loop(0, nh, greet_half, 0)
 
     def local(src, dst, i):
         one = pltpu.make_async_copy(src, dst, lsem.at[i])
@@ -48,7 +57,7 @@
 
     local_down = local(down_ref, down_v, 0)
     local_up = local(up_ref, up_v, 1)
-    local_c = local(cache_ref.at[:, g], r1.at[pl.ds(own * g, own)], 2)
+    local_c = [local(cache_ref.at[:, t, place], r1[t].at[pl.ds(own * g, own)], 8 + t) for t in range(2)]
     local_w = local(qkv_ref, wq.at[0], 3)
     local_wo = local(wo_ref, wo.at[0], 4)
     local_ff = local(ff_ref, wff.at[0], 5)
@@ -57,32 +66,37 @@
     index = jnp.zeros((8, 128), jnp.int32)
     for s in range(2 * seqs):
         index = jnp.where(lane8 == s, cidx_ref[0, s], index)
-    idxb[g] = index
+    idxb[place] = index
     bias = jnp.zeros((8, 128), f32)
     for h in range(half):
         bias = jnp.where(lane8 == h, bias_ref[h], bias)
     biasr[0] = bias
-    gates[0] = gate_ref[...]
-
-    pl.semaphore_wait(barrier, total - 1)
-
-    def cache_copy(p, slot):
+    zeros = jnp.zeros((128 - 2 * half, gate_ref.shape[2]), f32)
+    gates[0] = jnp.concatenate([gate_ref[0].astype(f32), gate_ref[1].astype(f32), zeros], axis=0).astype(bf16)
+
+    pl.semaphore_wait(barrier, n - 1 + nh)
+
+    def cache_copy(t, p, slot):
         return pltpu.make_async_remote_copy(
-            src_ref=cache_ref.at[:, p], dst_ref=r1.at[pl.ds(own * slot, own)],
-            send_sem=s1.at[p], recv_sem=t1.at[slot], device_id=(p, c), device_id_type=MESH)
-
-    def index_copy(p, slot):
+            src_ref=cache_ref.at[:, t, lax.rem(p, nh)], dst_ref=r1[t].at[pl.ds(own * slot, own)],
+            send_sem=s1.at[t * n + p], recv_sem=t1.at[t * n + slot], device_id=(p, c), device_id_type=MESH)
+
+    def index_copy(q, slot):
         return pltpu.make_async_remote_copy(
-            src_ref=idxb.at[g], dst_ref=idxb.at[slot],
-            send_sem=si.at[p], recv_sem=ti.at[slot], device_id=(p, c), device_id_type=MESH)
-
-    def first(k, carry):
-        p = lax.rem(g + k, n)
-        index_copy(p, g).start()
-        cache_copy(p, g).start()
-        return carry
-
-    lax.fori_loop(1, n, first, 0)
+            src_ref=idxb.at[place], dst_ref=idxb.at[slot],
+            send_sem=si.at[q], recv_sem=ti.at[slot], device_id=(start + q, c), device_id_type=MESH)
+
+    def send_index(k, carry):
+        index_copy(lax.rem(place + k, nh), place).start()
+        return carry
+
+    lax.fori_loop(1, nh, send_index, 0)
+    for t in range(2):
+        def first(k, carry, t=t):
+            cache_copy(t, lax.rem(g + k, n), g).start()
+            return carry
+
+        lax.fori_loop(1, n, first, 0)
 
     pairs = []
 
@@ -171,41 +185,60 @@
         levels.append(level)
         levels_t.append(jnp.transpose(level))
 
-    local_c.wait()
-
-    def first_wait(k, carry):
-        p = lax.rem(g + k, n)
-        index_copy(p, p).wait_recv()
-        cache_copy(p, p).wait_recv()
-        return carry
-
-    lax.fori_loop(1, n, first_wait, 0)
-    local(idxb, idxs, 6).wait()
-
-    def pick(p):
+    def index_wait(k, carry):
+        q = lax.rem(place + k, nh)
+        index_copy(q, q).wait_recv()
+        return carry
+
+    def pick(t, q):
         for b in range(2):
             for j in range(seqs):
-                i = idxs[p, 0, b * seqs + j]
-                piece = r1[jnp.minimum(i, own * n - 1)]
-                stage[p, b, j] = jnp.where(i < own * n, piece, jnp.zeros_like(piece))
-
-    def second_copy(d, slot_c, slot_g):
+                i = idxs[q, 0, b * seqs + j]
+                piece = r1[t][jnp.minimum(i, own * n - 1)]
+                stage[t, q, b, j] = jnp.where(i < own * n, piece, jnp.zeros_like(piece))
+
+    def second_copy(t, q, core, slot, at):
         return pltpu.make_async_remote_copy(
-            src_ref=stage.at[d // 2, lax.rem(d, 2)], dst_ref=r2.at[slot_c, slot_g],
-            send_sem=s2.at[d], recv_sem=t2.at[slot_c * n + slot_g],
-            device_id=(d // 2, lax.rem(d, 2)), device_id_type=MESH)
-
-    def second(k, carry):
-        p = lax.rem(g + k, n)
-        pick(p)
-        second_copy(p * 2 + c, 0, g).start()
-        second_copy(p * 2 + other, 1, g).start()
-        return carry
-
-    lax.fori_loop(1, n, second, 0)
-    pick(g)
-    second_copy(g * 2 + other, 1, g).start()
-    keep = local(stage.at[g, c], r2.at[0, g], 7)
+            src_ref=stage.at[t, q, core], dst_ref=r2.at[t, slot, at],
+            send_sem=s2.at[(t * nh + q) * 2 + core], recv_sem=t2.at[(t * 2 + slot) * nh + at],
+            device_id=(start + q, core), device_id_type=MESH)
+
+    def second_step(t):
+        local_c[t].wait()
+
+        def first_wait(k, carry):
+            p = lax.rem(g + k, n)
+            cache_copy(t, p, p).wait_recv()
+            return carry
+
+        lax.fori_loop(1, n, first_wait, 0)
+
+        def second(k, carry):
+            q = lax.rem(place + k, nh)
+            pick(t, q)
+            second_copy(t, q, c, 0, place).start()
+            second_copy(t, q, other, 1, place).start()
+            return carry
+
+        lax.fori_loop(1, nh, second, 0)
+        pick(t, place)
+        second_copy(t, place, other, 1, place).start()
+        return local(stage.at[t, place, c], r2.at[t, 0, place], 6 + t)
+
+    def second_wait(t):
+        def one(k, carry):
+            q = lax.rem(place + k, nh)
+            second_copy(t, q, c, 0, q).wait_recv()
+            second_copy(t, q, other, 1, q).wait_recv()
+            return carry
+
+        lax.fori_loop(1, nh, one, 0)
+        second_copy(t, place, other, 1, place).wait_recv()
+        keep[t].wait()
+
+    lax.fori_loop(1, nh, index_wait, 0)
+    local(idxb, idxs, 2).wait()
+    keep = [second_step(0)]
 
     scale = 1.0 / math.sqrt(dh)
 
@@ -216,7 +249,7 @@
         masked = jnp.where(allowed, scores, -jnp.inf)
         peak = jnp.max(masked, axis=1, keepdims=True)
         weights = jnp.exp(masked - peak)
-        probs = (weights / jnp.sum(weights, axis=1, keepdims=True)).astype(bf16)
+        probs = (weights * (1.0 / jnp.sum(weights, axis=1, keepdims=True))).astype(bf16)
         att_s[:, cols] = jnp.dot(probs, v_s[:, cols], preferred_element_type=f32)
         gap = jnp.where(allowed, levels[b][:, i:i + 1] - levels_t[b][i:i + 1, :], -jnp.inf)
         memory_w = (scores * jnp.exp(gap)).astype(bf16)
@@ -230,33 +263,33 @@
     q_s[:, cols] = (q + jnp.dot(low, upr[...], preferred_element_type=f32)).astype(bf16)
     k_s[:, cols] = jnp.dot(normed, wq[1, 1], preferred_element_type=f32).astype(bf16)
     v_s[:, cols] = jnp.dot(normed, wq[1, 2], preferred_element_type=f32).astype(bf16)
-    for h in range(half, 2 * half):
+    for h in range(half, half + half // 2):
         attend(h)
-
-    keep.wait()
-
-    def second_wait(k, carry):
-        p = lax.rem(g + k, n)
-        second_copy(p * 2 + c, 0, p).wait_recv()
-        second_copy(p * 2 + other, 1, p).wait_recv()
-        return carry
-
-    lax.fori_loop(1, n, second_wait, 0)
-    second_copy(g * 2 + other, 1, g).wait_recv()
-
-    per_head = n // half
-    for h in range(2 * half):
+    keep.append(second_step(1))
+    for h in range(half + half // 2, 2 * half):
+        attend(h)
+
+    per_head = 2 * nh // half
+
+    def recall(b, i):
+        h = b * half + i
+        t, at = i // (half // 2), (i % (half // 2)) * per_head
         cols = pl.ds(h * dh, dh)
-        b, i = h // half, h % half
         q = q_s[:, cols]
         carried = jnp.zeros((rows, dh), f32)
         for j in range(seqs):
-            state = r2[b, i * per_head:(i + 1) * per_head, j]
+            state = r2[t, b, at:at + per_head, j]
             state = state.astype(f32).reshape(dh, dh).astype(bf16)
             carried = jnp.where(seg_wide == j, jnp.dot(q, state, preferred_element_type=f32), carried)
         recalled = carried * jnp.exp(levels[b][:, i:i + 1]) + intra_s[:, cols]
         factor = lax.rsqrt(jnp.mean(recalled * recalled, axis=1, keepdims=True) + epsilon)
         head_s[:, cols] = (att_s[:, cols] + mixes[b][:, half + i:half + i + 1] * recalled * factor).astype(bf16)
+
+    for t in range(2):
+        second_wait(t)
+        for b in range(2):
+            for i in range(t * (half // 2), (t + 1) * (half // 2)):
+                recall(b, i)
 
     local_wo.wait()
     pair_wo.wait_recv()
@@ -265,7 +298,6 @@
     mixed = (tok_ref[...].astype(f32) + proj).astype(bf16).astype(f32)
     factor = lax.rsqrt(jnp.mean(mixed * mixed, axis=-1, keepdims=True) + epsilon)
     normed_two = (mixed * factor * gain_ref[1:2, :]).astype(bf16)
-    feed = mixed
     local_ff.wait()
     for b in range(2):
         if b == 1:
@@ -277,19 +309,28 @@
         hidden = (gate / (1.0 + jnp.exp(-gate)) * upper).astype(bf16)
         if b == 1:
             pair_ff[2].wait_recv()
-        feed = feed + lax.dot_general(hidden, wff[b, 2], nt, preferred_element_type=f32)
-    out_ref[...] = feed.astype(bf16)
-
-    def drain(k, carry):
+        down_t = lax.dot_general(wff[b, 2], hidden, nt, preferred_element_type=f32)
+        feed_t = down_t if b == 0 else feed_t + down_t
+    out_ref[...] = (mixed + jnp.transpose(feed_t)).astype(bf16)
+
+    def drain_first(k, carry):
         p = lax.rem(g + k, n)
-        index_copy(p, g).wait_send()
-        cache_copy(p, g).wait_send()
-        second_copy(p * 2 + c, 0, g).wait_send()
-        second_copy(p * 2 + other, 1, g).wait_send()
-        return carry
-
-    lax.fori_loop(1, n, drain, 0)
-    second_copy(g * 2 + other, 1, g).wait_send()
+        cache_copy(0, p, g).wait_send()
+        cache_copy(1, p, g).wait_send()
+        return carry
+
+    def drain_second(k, carry):
+        q = lax.rem(place + k, nh)
+        index_copy(q, place).wait_send()
+        for t in range(2):
+            second_copy(t, q, c, 0, place).wait_send()
+            second_copy(t, q, other, 1, place).wait_send()
+        return carry
+
+    lax.fori_loop(1, n, drain_first, 0)
+    lax.fori_loop(1, nh, drain_second, 0)
+    for t in range(2):
+        second_copy(t, place, other, 1, place).wait_send()
     for one in pairs:
         one.wait_send()
 
@@ -307,12 +348,10 @@
     head_cols = query_key_value_weight.shape[2]
     dh = head_cols // half
     own = caches.shape[0]
+    nh = n // 2
     piece = half * dh // n
     base = seqs * rank
     bf16, f32 = jnp.bfloat16, jnp.float32
-
-    gate = head_gate_weight.transpose(0, 2, 1).reshape(2 * half, width)
-    gate = jnp.pad(gate, ((0, 128 - 2 * half), (0, 0)))
 
     vmem = pl.BlockSpec(memory_space=pltpu.VMEM)
     smem = pl.BlockSpec(memory_space=pltpu.SMEM)
@@ -337,26 +376,27 @@
             pltpu.VMEM((2,) + head_output_weight.shape, bf16),
             pltpu.VMEM((2,) + feedforward_weight.shape, bf16),
             pltpu.VMEM((own * n, piece, dh), bf16),
-            pltpu.VMEM((n, 8, 128), jnp.int32),
-            pltpu.SMEM((n, 8, 128), jnp.int32),
-            pltpu.VMEM((n, 2, seqs, piece, dh), bf16),
-            pltpu.VMEM((2, n, seqs, piece, dh), bf16),
+            pltpu.VMEM((own * n, piece, dh), bf16),
+            pltpu.VMEM((nh, 8, 128), jnp.int32),
+            pltpu.SMEM((nh, 8, 128), jnp.int32),
+            pltpu.VMEM((2, nh, 2, seqs, piece, dh), bf16),
+            pltpu.VMEM((2, 2, nh, seqs, piece, dh), bf16),
             pltpu.VMEM((rows, wide), bf16),
             pltpu.VMEM((rows, wide), bf16),
             pltpu.VMEM((rows, wide), bf16),
             pltpu.VMEM((rows, wide), f32),
             pltpu.VMEM((rows, wide), f32),
             pltpu.VMEM((rows, wide), bf16),
-            dma((n,)), dma((n,)), dma((n,)), dma((n,)), dma((2 * n,)), dma((2 * n,)),
-            dma((10,)), dma((10,)), dma((8,)),
+            dma((2 * n,)), dma((2 * n,)), dma((nh,)), dma((nh,)), dma((4 * nh,)), dma((4 * nh,)),
+            dma((10,)), dma((10,)), dma((10,)),
         ],
         compiler_params=pltpu.CompilerParams(
             collective_id=0, has_side_effects=True, vmem_limit_bytes=56 * 2**20),
         cost_estimate=pl.CostEstimate(flops=7 * 10**9, bytes_accessed=3 * 10**7, transcendentals=10**6),
     )(
         lengths, request_adapter_index, request_cache_index, decay_logit_bias, tokens, norm_gain_pair,
-        gate, adapter_down_factor.transpose(0, 2, 1), adapter_up_factor, query_key_value_weight,
-        caches.reshape(own, n, piece, dh), head_output_weight, feedforward_weight,
+        head_gate_weight.transpose(0, 2, 1), adapter_down_factor.transpose(0, 2, 1), adapter_up_factor, query_key_value_weight,
+        caches.reshape(own, 2, nh, piece, dh), head_output_weight, feedforward_weight,
     )
 
 

time: 53.9 us -> 50.1 us (0.929)
  the two profiles are of different devices: /device:TPU:29 before, /device:TPU:0 now
where the time goes in v4:
time: 50.1 us; the launch traced here: 49.9 us
  Pallas kernels  48 us (96%)
  local copies, waits for them, and re-layouts  1.87 us (4%)
    pallas_call x1, Pallas kernels, on_device(): pl.pallas_call(functools.partial(mix_kernel, n, seqs, rank, half, dh), ou...  48 us
    unnamed x1, local copies, waits for them, and re-layouts  1.87 us

profile of v4, /device:TPU:0, one launch (start us, length us, event | category | flops | bytes accessed | tf_op | source)
XLA Modules:
  0.0 49.9 jit_solution(18069887162421642080)
XLA Ops:
  0.0 48.0 %shard_map.127 = bf16[256,1024]{1,0:T(8,128)(2,1)} custom-call(s32[1,2,3]{2,1,0:T(2,128)} %lens_ref.1, s32[1,6]{1,0:T(1,128)} %aidx_ref.1, s32[1,6]{1,0:T(1,128)} %cidx_ref.1, f32[4]{0:T(128)} %bias_ref.1, bf16[256,1024]{1,0:T(8,128)(2,1)} %tok_ref.1, f32[2,1024]{1,0:T(2,128)} %gain_ref.1, bf16[2,4,1024]{2,1,0:T(4,128)(2,1)} %bitcast.5, ...), custom_call_target="tpu_custom_call" | custom-call | flops 7000000000 | bytes 30000000 | tf_op jit(solution)/shard_map/pallas_call | solution.py:361
  48.1 1.9 %copy.15 = bf16[256,1024]{1,0:T(8,128)(2,1)} copy(bf16[256,1024]{1,0:T(8,128)(2,1)} %shard_map.127) | data formatting | bytes 1048576

commit v5 on v4

--- a/solution.py
+++ b/solution.py
@@ -263,10 +263,8 @@
     q_s[:, cols] = (q + jnp.dot(low, upr[...], preferred_element_type=f32)).astype(bf16)
     k_s[:, cols] = jnp.dot(normed, wq[1, 1], preferred_element_type=f32).astype(bf16)
     v_s[:, cols] = jnp.dot(normed, wq[1, 2], preferred_element_type=f32).astype(bf16)
-    for h in range(half, half + half // 2):
-        attend(h)
     keep.append(second_step(1))
-    for h in range(half + half // 2, 2 * half):
+    for h in range(half, 2 * half):
         attend(h)
 
     per_head = 2 * nh // half

time: 50.1 us -> 50.1 us (level)
  no operation moved by 1% of the time
where the time goes in v5:
time: 50.1 us; the launch traced here: 49.9 us
  Pallas kernels  48 us (96%)
  local copies, waits for them, and re-layouts  1.87 us (4%)
    pallas_call x1, Pallas kernels, on_device(): pl.pallas_call(functools.partial(mix_kernel, n, seqs, rank, half, dh), ou...  48 us
    unnamed x1, local copies, waits for them, and re-layouts  1.87 us

profile of v5, /device:TPU:0, one launch (start us, length us, event | category | flops | bytes accessed | tf_op | source)
XLA Modules:
  0.0 49.9 jit_solution(17424246327342068637)
XLA Ops:
  0.0 48.0 %shard_map.127 = bf16[256,1024]{1,0:T(8,128)(2,1)} custom-call(s32[1,2,3]{2,1,0:T(2,128)} %lens_ref.1, s32[1,6]{1,0:T(1,128)} %aidx_ref.1, s32[1,6]{1,0:T(1,128)} %cidx_ref.1, f32[4]{0:T(128)} %bias_ref.1, bf16[256,1024]{1,0:T(8,128)(2,1)} %tok_ref.1, f32[2,1024]{1,0:T(2,128)} %gain_ref.1, bf16[2,4,1024]{2,1,0:T(4,128)(2,1)} %bitcast.5, ...), custom_call_target="tpu_custom_call" | custom-call | flops 7000000000 | bytes 30000000 | tf_op jit(solution)/shard_map/pallas_call | solution.py:359
  48.0 1.9 %copy.15 = bf16[256,1024]{1,0:T(8,128)(2,1)} copy(bf16[256,1024]{1,0:T(8,128)(2,1)} %shard_map.127) | data formatting | bytes 1048576

commit v6 on v5

--- a/solution.py
+++ b/solution.py
@@ -283,17 +283,20 @@
         factor = lax.rsqrt(jnp.mean(recalled * recalled, axis=1, keepdims=True) + epsilon)
         head_s[:, cols] = (att_s[:, cols] + mixes[b][:, half + i:half + i + 1] * recalled * factor).astype(bf16)
 
+    local_wo.wait()
+    pair_wo.wait_recv()
+    mid = width // 2
+    proj = tok_ref[...].astype(f32)
     for t in range(2):
         second_wait(t)
         for b in range(2):
             for i in range(t * (half // 2), (t + 1) * (half // 2)):
                 recall(b, i)
-
-    local_wo.wait()
-    pair_wo.wait_recv()
-    proj = jnp.dot(head_s[:, :width], wo[0], preferred_element_type=f32)
-    proj = proj + jnp.dot(head_s[:, width:], wo[1], preferred_element_type=f32)
-    mixed = (tok_ref[...].astype(f32) + proj).astype(bf16).astype(f32)
+        for b in range(2):
+            at = b * width + t * mid
+            proj = proj + jnp.dot(
+                head_s[:, at:at + mid], wo[b, t * mid:(t + 1) * mid, :], preferred_element_type=f32)
+    mixed = proj.astype(bf16).astype(f32)
     factor = lax.rsqrt(jnp.mean(mixed * mixed, axis=-1, keepdims=True) + epsilon)
     normed_two = (mixed * factor * gain_ref[1:2, :]).astype(bf16)
     local_ff.wait()

time: 50.1 us -> 50 us (level)
  no operation moved by 1% of the time
where the time goes in v6:
time: 50 us; the launch traced here: 49.8 us
  Pallas kernels  47.9 us (96%)
  local copies, waits for them, and re-layouts  1.87 us (4%)
    pallas_call x1, Pallas kernels, on_device(): pl.pallas_call(functools.partial(mix_kernel, n, seqs, rank, half, dh), ou...  47.9 us
    unnamed x1, local copies, waits for them, and re-layouts  1.87 us

profile of v6, /device:TPU:0, one launch (start us, length us, event | category | flops | bytes accessed | tf_op | source)
XLA Modules:
  0.0 49.8 jit_solution(17294233754804222707)
XLA Ops:
  0.0 47.9 %shard_map.127 = bf16[256,1024]{1,0:T(8,128)(2,1)} custom-call(s32[1,2,3]{2,1,0:T(2,128)} %lens_ref.1, s32[1,6]{1,0:T(1,128)} %aidx_ref.1, s32[1,6]{1,0:T(1,128)} %cidx_ref.1, f32[4]{0:T(128)} %bias_ref.1, bf16[256,1024]{1,0:T(8,128)(2,1)} %tok_ref.1, f32[2,1024]{1,0:T(2,128)} %gain_ref.1, bf16[2,4,1024]{2,1,0:T(4,128)(2,1)} %bitcast.5, ...), custom_call_target="tpu_custom_call" | custom-call | flops 7000000000 | bytes 30000000 | tf_op jit(solution)/shard_map/pallas_call | solution.py:362
  47.9 1.9 %copy.15 = bf16[256,1024]{1,0:T(8,128)(2,1)} copy(bf16[256,1024]{1,0:T(8,128)(2,1)} %shard_map.127) | data formatting | bytes 1048576
